TPU v7x, 256 devices: a whole 4x4x8 slice. The times are simulated.
256 devices in a mesh: space: 32 (over z_hi, x, core), chan: 8 (over y, z_lo).
Axes of the slice: x: 4, y: 4, z: 8 (z_hi: 4, z_lo: 2; z = z_hi * 2 + z_lo), core: 2. Of those that a mesh axis runs over, the one named last changes fastest.
Arguments:
- field: bfloat16 [256, 8, 4096], P('chan', None, 'space'), may hold values from -6 to 6
- first_weight: bfloat16 [256, 9, 256], P('chan'), may hold values from -0.125 to 0.125
- second_weight: bfloat16 [256, 9, 256], P('chan'), may hold values from -0.125 to 0.125
- cotangent: bfloat16 [256, 8, 4096], P('chan', None, 'space'), may hold values from -6 to 6
Outputs:
- field_grad: bfloat16 [256, 8, 4096], P('chan', None, 'space')
- first_grad: float32 [256, 9, 256], P('chan')
- second_grad: float32 [256, 9, 256], P('chan')
All inputs are finite; a program needn't handle non-finite values.
Results may differ from a plain program's by a relative error of at most 0.0053.
Values may be sent and summed in bfloat16 or wider, within the bound.
A program may use at most 64 MiB of HBM per device.

v0:
```python
import math

import jax
import jax.numpy as jnp
from jax import lax
from jax.sharding import PartitionSpec as P


def with_halo(block, sides, width):
    for axis, dim in sides:
        count = lax.axis_size(axis)
        forward = [(i, i + 1) for i in range(count - 1)]
        forward.append((count - 1, 0))
        backward = [(target, source) for source, target in forward]
        low = lax.ppermute(
            lax.slice_in_dim(block, block.shape[dim] - width, None, axis=dim), axis, forward
        )
        high = lax.ppermute(lax.slice_in_dim(block, 0, width, axis=dim), axis, backward)
        block = jnp.concatenate([low, block, high], axis=dim)
    return block


def pad_rows(values):
    return jnp.pad(values, ((0, 0), (1, 1), (0, 0)))


def widen(values):
    return with_halo(values, (("space", 2),), 2)


def collect(values):
    return lax.all_gather(values, "chan", axis=0, tiled=True)


def conv_forward(padded, weight):
    height = padded.shape[1] - 2
    length = padded.shape[2] - 2
    total = jnp.zeros((weight.shape[0], height, length), jnp.float32)
    for tap_row in range(3):
        for tap_col in range(3):
            window = padded[:, tap_row : tap_row + height, tap_col : tap_col + length]
            total = total + jnp.einsum(
                "oi,irc->orc",
                weight[:, 3 * tap_row + tap_col, :],
                window,
                preferred_element_type=jnp.float32,
            )
    return total


def conv_back(padded, weight):
    height = padded.shape[1] - 2
    length = padded.shape[2] - 2
    total = jnp.zeros((weight.shape[2], height, length), jnp.float32)
    for tap_row in range(3):
        for tap_col in range(3):
            window = padded[
                :, 2 - tap_row : 2 - tap_row + height, 2 - tap_col : 2 - tap_col + length
            ]
            total = total + jnp.einsum(
                "oi,orc->irc",
                weight[:, 3 * tap_row + tap_col, :],
                window,
                preferred_element_type=jnp.float32,
            )
    return total


def reduce_back(padded, weight):
    return lax.psum_scatter(conv_back(padded, weight), "chan", scatter_dimension=0, tiled=True)


def weight_grad(upstream, padded):
    height = upstream.shape[1]
    length = upstream.shape[2]
    pieces = []
    for tap_row in range(3):
        for tap_col in range(3):
            window = padded[:, tap_row : tap_row + height, tap_col : tap_col + length]
            pieces.append(
                jnp.einsum("orc,irc->oi", upstream, window, preferred_element_type=jnp.float32)
            )
    return jnp.stack(pieces, axis=1)


def smooth_gelu(values):
    return jax.nn.gelu(values, approximate=True)


def resample(extended):
    lower = jnp.pad(extended, ((0, 0), (0, 1), (0, 0)))
    top_left = lower[:, :-1, :-1]
    top_right = lower[:, :-1, 1:]
    low_left = lower[:, 1:, :-1]
    low_right = lower[:, 1:, 1:]
    even_even = smooth_gelu(top_left)
    even_odd = smooth_gelu((top_left + top_right) * 0.5)
    odd_even = smooth_gelu((top_left + low_left) * 0.5)
    odd_odd = smooth_gelu((top_left + top_right + low_left + low_right) * 0.25)
    row_even = (even_odd[:, :, :-1] + 2.0 * even_even[:, :, 1:] + even_odd[:, :, 1:]) * 0.25
    row_odd = (odd_odd[:, :, :-1] + 2.0 * odd_even[:, :, 1:] + odd_odd[:, :, 1:]) * 0.25
    shifted = jnp.pad(row_odd, ((0, 0), (1, 0), (0, 0)))[:, :-1]
    return (shifted + 2.0 * row_even + row_odd) * 0.25


def split_plan(field, first_weight, second_weight, cotangent, grad_scale):
    field_all = collect(widen(field))
    field_pad = pad_rows(field_all[:, :, 1:-1])
    hidden = conv_forward(field_pad, first_weight).astype(jnp.bfloat16)
    hidden_wide = widen(hidden)
    smooth_values, pullback = jax.vjp(resample, hidden_wide.astype(jnp.float32))
    smooth = smooth_values[:, :, 1:-1].astype(jnp.bfloat16)
    smooth_all = collect(widen(smooth))
    smooth_pad = pad_rows(smooth_all[:, :, 1:-1])
    cot_wide = widen(cotangent)
    second_grad = weight_grad(cotangent, smooth_pad) * grad_scale
    smooth_sum = reduce_back(pad_rows(cot_wide[:, :, 1:-1]), second_weight)
    smooth_grad = smooth_sum.astype(jnp.bfloat16)
    grad_wide = widen(smooth_grad)
    hidden_full = pullback(grad_wide[:, :, 1:-1].astype(jnp.float32))[0]
    hidden_grad = hidden_full[:, :, 2:-2].astype(jnp.bfloat16)
    first_grad = weight_grad(hidden_grad, field_pad) * grad_scale
    hidden_grad_wide = widen(hidden_grad)
    field_sum = reduce_back(pad_rows(hidden_grad_wide[:, :, 1:-1]), first_weight)
    field_grad = (cotangent.astype(jnp.float32) + field_sum).astype(jnp.bfloat16)
    return (field_grad, first_grad, second_grad)


def on_device(field, first_weight, second_weight, cotangent):
    height = field.shape[1]
    length = field.shape[2]
    grad_scale = 1.0 / math.sqrt(height * length * lax.axis_size("space"))
    field_grad, first_grad, second_grad = split_plan(
        field, first_weight, second_weight, cotangent, grad_scale
    )
    first_grad, second_grad = lax.psum((first_grad, second_grad), "space")
    return (field_grad, first_grad, second_grad)


def solution(mesh):
    in_specs = (
        P("chan", None, "space"),
        P("chan", None, None),
        P("chan", None, None),
        P("chan", None, "space"),
    )
    out_specs = (P("chan", None, "space"), P("chan", None, None), P("chan", None, None))
    return jax.shard_map(
        on_device, mesh=mesh, in_specs=in_specs, out_specs=out_specs, check_vma=False
    )
```

profile of v0, /device:TPU:1, one launch (start us, length us, event | category | flops | bytes accessed | tf_op | source)
XLA Modules:
  0.0 502.2 jit_solution(2179057521103253307)
XLA Ops:
  7.2 0.9 copy.116
  8.2 2.7 collective-permute-start.4
  10.8 0.7 collective-permute-start.5
  11.6 0.8 copy.107
  12.5 1.1 collective-permute-start
  13.6 5.3 %collective-permute-start.1 = (bf16[32,8,2]{2,0,1:T(8,128)(2,1)S(1)}, bf16[32,8,2]{2,0,1:T(8,128)(2,1)S(1)}, u32[]{:S(2)}, u32[]{:S(2)}) collective-permute-start(bf16[32,8,2]{2,0,1:T(8,128)(2,1)S(1)} %get-tuple-element.40), channel_id=1, source_target_pairs={{8,0},{16,8},{24,16},{32,24},{40,32},{48,40},{56,48},{64,56},{72,6... | collective-permute-start | bytes 3080 | tf_op jit(solution)/shard_map/ppermute | solution.py:18
  18.9 1.2 fusion.128
  20.2 28.3 %all_gather.6 = bf16[256,8,132]{2,0,1:T(8,128)(2,1)S(1)} all-gather(bf16[32,8,132]{2,0,1:T(8,128)(2,1)S(1)} %pad_maximum_fusion.2), channel_id=1, replica_groups=mesh['space'=32,'chan'=8] {'chan'}, dimensions={0}, use_global_device_ids=true | all-gather | bytes 608256 | tf_op jit(solution)/shard_map/all_gather | solution.py:32
  49.6 1.0 convolution_add_fusion.16
  54.1 1.3 copy.114
  55.5 0.8 copy-done.2
  58.7 2.0 collective-permute-start.6
  60.7 8.7 %collective-permute-start.7 = (bf16[32,8,2]{2,0,1:T(8,128)(2,1)S(1)}, bf16[32,8,2]{2,0,1:T(8,128)(2,1)S(1)}, u32[]{:S(2)}, u32[]{:S(2)}) collective-permute-start(bf16[32,8,2]{2,0,1:T(8,128)(2,1)S(1)} %get-tuple-element.34), channel_id=1, source_target_pairs={{8,0},{16,8},{24,16},{32,24},{40,32},{48,40},{56,48},{64,56},{72,6... | collective-permute-start | bytes 3080 | tf_op jit(solution)/shard_map/ppermute | solution.py:18
  70.6 31.6 %reduce-scatter.3.cloned.1.call-done = f32[32,8,128]{2,1,0:T(8,128)} async-done(((f32[256,8,128]{2,1,0:T(8,128)}), f32[32,8,128]{2,1,0:T(8,128)}) %reduce-scatter.3.cloned.1.call-update) | async-done | bytes 131088 | tf_op jit(solution)/shard_map/reduce_scatter | solution.py:70
  102.3 0.9 convert_element_type.31
  103.3 6.6 %collective-permute-start.2 = (bf16[32,8,2]{2,1,0:T(8,128)(2,1)S(1)}, bf16[32,8,2]{2,1,0:T(8,128)(2,1)S(1)}, u32[]{:S(2)}, u32[]{:S(2)}) collective-permute-start(bf16[32,8,2]{2,1,0:T(8,128)(2,1)S(1)} %get-tuple-element.37), channel_id=1, source_target_pairs={{0,8},{8,16},{16,24},{24,32},{32,40},{40,48},{48,56},{56,64},{64,7... | collective-permute-start | bytes 3080 | tf_op jit(solution)/shard_map/ppermute | solution.py:15
  110.1 1.1 collective-permute-done.2
  111.2 2.4 collective-permute-done.3
  116.4 4.0 collective-permute-start.11
  120.4 6.0 %collective-permute-start.9 = (bf16[32,8,2]{2,0,1:T(8,128)(2,1)S(1)}, bf16[32,8,2]{2,0,1:T(8,128)(2,1)S(1)}, u32[]{:S(2)}, u32[]{:S(2)}) collective-permute-start(bf16[32,8,2]{2,0,1:T(8,128)(2,1)S(1)} %get-tuple-element.28), channel_id=1, source_target_pairs={{8,0},{16,8},{24,16},{32,24},{40,32},{48,40},{56,48},{64,56},{72,6... | collective-permute-start | bytes 3080 | tf_op jit(solution)/shard_map/ppermute | solution.py:18
  129.2 0.7 broadcast_multiply_fusion.1
  131.4 26.2 %all_gather.7 = bf16[256,8,132]{2,1,0:T(8,128)(2,1)S(1)} all-gather(bf16[32,8,132]{2,1,0:T(8,128)(2,1)S(1)} %pad_maximum_fusion.3), channel_id=1, replica_groups=mesh['space'=32,'chan'=8] {'chan'}, dimensions={0}, use_global_device_ids=true | all-gather | bytes 608256 | tf_op jit(solution)/shard_map/all_gather | solution.py:32
  158.8 0.9 fusion.19
  159.7 1.0 fusion.18
  163.1 1.3 copy.119
  164.5 0.9 copy-done.3
  168.0 0.7 broadcast_multiply_fusion
  168.8 42.2 %reduce-scatter.5.cloned.1.call-done = f32[32,8,128]{2,1,0:T(8,128)} async-done(((f32[256,8,128]{2,1,0:T(8,128)}), f32[32,8,128]{2,1,0:T(8,128)}) %reduce-scatter.5.cloned.1.call-update) | async-done | bytes 131088 | tf_op jit(solution)/shard_map/reduce_scatter | solution.py:70
  211.0 1.5 add_convert_fusion.1
  212.5 279.8 %all-reduce.20.cloned.1.call-done = (f32[32,9,256]{2,0,1:T(8,128)}, f32[32,9,256]{2,0,1:T(8,128)}) async-done(((f32[32,9,256]{2,0,1:T(8,128)}, f32[32,9,256]{2,0,1:T(8,128)}), (f32[32,9,256]{2,0,1:T(8,128)}, f32[32,9,256]{2,0,1:T(8,128)})) %all-reduce.20.cloned.1.call-update) | async-done | bytes 589840 | tf_op jit(solution)/shard_map/psum | solution.py:136
  492.3 1.7 copy.188
  494.0 1.7 copy.189
  (97 shorter events, 22.1 us)
Async XLA Ops:
  7.2 95.1 %reduce-scatter.3.cloned.1.call-start = ((), (), s32[]{:S(2)}) async-start(), calls=%async_computation.2 | async-start | bytes 1179648 | tf_op jit(solution)/shard_map/reduce_scatter | solution.py:70
  8.2 11.9 %collective-permute-start.4 = (bf16[32,8,2]{2,0,1:T(8,128)(2,1)S(1)}, bf16[32,8,2]{2,0,1:T(8,128)(2,1)S(1)}, u32[]{:S(2)}, u32[]{:S(2)}) collective-permute-start(bf16[32,8,2]{2,0,1:T(8,128)(2,1)S(1)} %get-tuple-element.35), channel_id=1, source_target_pairs={{0,8},{8,16},{16,24},{24,32},{32,40},{40,48},{48,56},{56,64},{64,7... | collective-permute-start | bytes 3080 | tf_op jit(solution)/shard_map/ppermute | solution.py:15
  10.8 9.3 %collective-permute-start.5 = (bf16[32,8,2]{2,0,1:T(8,128)(2,1)S(1)}, bf16[32,8,2]{2,0,1:T(8,128)(2,1)S(1)}, u32[]{:S(2)}, u32[]{:S(2)}) collective-permute-start(bf16[32,8,2]{2,0,1:T(8,128)(2,1)S(1)} %get-tuple-element.36), channel_id=1, source_target_pairs={{8,0},{16,8},{24,16},{32,24},{40,32},{48,40},{56,48},{64,56},{72,6... | collective-permute-start | bytes 3080 | tf_op jit(solution)/shard_map/ppermute | solution.py:18
  12.5 38.1 %collective-permute-start = (bf16[32,8,2]{2,0,1:T(8,128)(2,1)S(1)}, bf16[32,8,2]{2,0,1:T(8,128)(2,1)S(1)}, u32[]{:S(2)}, u32[]{:S(2)}) collective-permute-start(bf16[32,8,2]{2,0,1:T(8,128)(2,1)S(1)} %get-tuple-element.39), channel_id=1, source_target_pairs={{0,8},{8,16},{16,24},{24,32},{32,40},{40,48},{48,56},{56,64},{64,7... | collective-permute-start | bytes 3080 | tf_op jit(solution)/shard_map/ppermute | solution.py:15
  13.6 37.0 %collective-permute-start.1 = (bf16[32,8,2]{2,0,1:T(8,128)(2,1)S(1)}, bf16[32,8,2]{2,0,1:T(8,128)(2,1)S(1)}, u32[]{:S(2)}, u32[]{:S(2)}) collective-permute-start(bf16[32,8,2]{2,0,1:T(8,128)(2,1)S(1)} %get-tuple-element.40), channel_id=1, source_target_pairs={{8,0},{16,8},{24,16},{32,24},{40,32},{48,40},{56,48},{64,56},{72,6... | collective-permute-start | bytes 3080 | tf_op jit(solution)/shard_map/ppermute | solution.py:18
  48.5 0.9 copy-start.1
  49.6 1.2 copy-start.4
  55.4 0.9 copy-start.2
  55.4 155.5 %reduce-scatter.5.cloned.1.call-start = ((), (), s32[]{:S(2)}) async-start(), calls=%async_computation.3 | async-start | bytes 1179648 | tf_op jit(solution)/shard_map/reduce_scatter | solution.py:70
  58.7 11.3 %collective-permute-start.6 = (bf16[32,8,2]{2,0,1:T(8,128)(2,1)S(1)}, bf16[32,8,2]{2,0,1:T(8,128)(2,1)S(1)}, u32[]{:S(2)}, u32[]{:S(2)}) collective-permute-start(bf16[32,8,2]{2,0,1:T(8,128)(2,1)S(1)} %get-tuple-element.33), channel_id=1, source_target_pairs={{0,8},{8,16},{16,24},{24,32},{32,40},{40,48},{48,56},{56,64},{64,7... | collective-permute-start | bytes 3080 | tf_op jit(solution)/shard_map/ppermute | solution.py:15
  60.7 9.6 %collective-permute-start.7 = (bf16[32,8,2]{2,0,1:T(8,128)(2,1)S(1)}, bf16[32,8,2]{2,0,1:T(8,128)(2,1)S(1)}, u32[]{:S(2)}, u32[]{:S(2)}) collective-permute-start(bf16[32,8,2]{2,0,1:T(8,128)(2,1)S(1)} %get-tuple-element.34), channel_id=1, source_target_pairs={{8,0},{16,8},{24,16},{32,24},{40,32},{48,40},{56,48},{64,56},{72,6... | collective-permute-start | bytes 3080 | tf_op jit(solution)/shard_map/ppermute | solution.py:18
  103.3 7.9 %collective-permute-start.2 = (bf16[32,8,2]{2,1,0:T(8,128)(2,1)S(1)}, bf16[32,8,2]{2,1,0:T(8,128)(2,1)S(1)}, u32[]{:S(2)}, u32[]{:S(2)}) collective-permute-start(bf16[32,8,2]{2,1,0:T(8,128)(2,1)S(1)} %get-tuple-element.37), channel_id=1, source_target_pairs={{0,8},{8,16},{16,24},{24,32},{32,40},{40,48},{48,56},{56,64},{64,7... | collective-permute-start | bytes 3080 | tf_op jit(solution)/shard_map/ppermute | solution.py:15
  109.9 3.7 collective-permute-start.3
  116.3 14.9 %collective-permute-start.10 = (bf16[32,8,2]{2,0,1:T(8,128)(2,1)S(1)}, bf16[32,8,2]{2,0,1:T(8,128)(2,1)S(1)}, u32[]{:S(2)}, u32[]{:S(2)}) collective-permute-start(bf16[32,8,2]{2,0,1:T(8,128)(2,1)S(1)} %get-tuple-element.29), channel_id=1, source_target_pairs={{0,8},{8,16},{16,24},{24,32},{32,40},{40,48},{48,56},{56,64},{64,7... | collective-permute-start | bytes 3080 | tf_op jit(solution)/shard_map/ppermute | solution.py:15
  116.4 14.8 %collective-permute-start.11 = (bf16[32,8,2]{2,0,1:T(8,128)(2,1)S(1)}, bf16[32,8,2]{2,0,1:T(8,128)(2,1)S(1)}, u32[]{:S(2)}, u32[]{:S(2)}) collective-permute-start(bf16[32,8,2]{2,0,1:T(8,128)(2,1)S(1)} %get-tuple-element.30), channel_id=1, source_target_pairs={{8,0},{16,8},{24,16},{32,24},{40,32},{48,40},{56,48},{64,56},{72,6... | collective-permute-start | bytes 3080 | tf_op jit(solution)/shard_map/ppermute | solution.py:18
  120.4 9.7 %collective-permute-start.8 = (bf16[32,8,2]{2,0,1:T(8,128)(2,1)S(1)}, bf16[32,8,2]{2,0,1:T(8,128)(2,1)S(1)}, u32[]{:S(2)}, u32[]{:S(2)}) collective-permute-start(bf16[32,8,2]{2,0,1:T(8,128)(2,1)S(1)} %get-tuple-element.27), channel_id=1, source_target_pairs={{0,8},{8,16},{16,24},{24,32},{32,40},{40,48},{48,56},{56,64},{64,7... | collective-permute-start | bytes 3080 | tf_op jit(solution)/shard_map/ppermute | solution.py:15
  120.4 9.7 %collective-permute-start.9 = (bf16[32,8,2]{2,0,1:T(8,128)(2,1)S(1)}, bf16[32,8,2]{2,0,1:T(8,128)(2,1)S(1)}, u32[]{:S(2)}, u32[]{:S(2)}) collective-permute-start(bf16[32,8,2]{2,0,1:T(8,128)(2,1)S(1)} %get-tuple-element.28), channel_id=1, source_target_pairs={{8,0},{16,8},{24,16},{32,24},{40,32},{48,40},{56,48},{64,56},{72,6... | collective-permute-start | bytes 3080 | tf_op jit(solution)/shard_map/ppermute | solution.py:18
  158.0 0.8 copy-start
  164.4 1.0 copy-start.3
  164.4 327.9 %all-reduce.20.cloned.1.call-start = ((), (), s32[]{:S(2)}) async-start(), calls=%async_computation.4 | async-start | bytes 1179648 | tf_op jit(solution)/shard_map/psum | solution.py:136
Sparse Core Ops, SparseCore 0:
  55.6 46.6 reduce-scatter.2
  164.6 46.3 reduce-scatter.4
  214.2 278.0 all-reduce.19
where the time goes:
time: 503 us; the launch traced here: 502 us
  waiting for transfers between devices  358 us (71%)
  blocking collectives  54.4 us (11%)
  starting transfers between devices  37.2 us (7%)
  matrix products  18.6 us (4%)
  between operations  14.2 us (3%)
  local copies, waits for them, and re-layouts  12.9 us (3%)
  other arithmetic  6.88 us (1%)
    psum x1, waiting for transfers between devices, on_device(): first_grad, second_grad = lax.psum((first_grad, second_grad), 'space')  280 us
    reduce_scatter x2, waiting for transfers between devices, reduce_back(): lax.psum_scatter(conv_back(padded, weight), 'chan', scatter_dimension=0,...  73.8 us
    all_gather x2, blocking collectives, collect(): return lax.all_gather(values, 'chan', axis=0, tiled=True)  54.4 us
    ppermute x6, starting transfers between devices, with_halo(): lax.ppermute(lax.slice_in_dim(block, 0, width, axis=dim), axis, backward)  24.7 us
    ppermute x6, starting transfers between devices, with_halo(): lax.ppermute(lax.slice_in_dim(block, block.shape[dim] - width, None, axis...  12.4 us
  transfers between devices with their start and end apart: 15, of which 7 were waited for; matrix products, arithmetic and copies ran while one was open for 3% of the time, Pallas kernels for 0%

commit v1 on v0

v1 whole, which is shorter than its diff:
```python
import math

import jax
import jax.numpy as jnp
from jax import lax
from jax.experimental import pallas as pl
from jax.experimental.pallas import tpu as pltpu
from jax.sharding import PartitionSpec as P

MESH = pl.DeviceIdType.MESH
F32 = jnp.float32
BF16 = jnp.bfloat16
CH = 8
SP = 32
NB = 32
ROWS = 8
LANES = 128
PEERS = SP // 2
TILES = 3
TAPS = [(p, q) for p in (-1, 0, 1) for q in (-1, 0, 1)]


def tap(p, q):
    return 3 * (p + 1) + q + 1


def lane_ids(shape):
    return lax.broadcasted_iota(jnp.int32, shape, len(shape) - 1)


def roll(values, amount):
    amount = amount % LANES
    if amount == 0:
        return values
    return pltpu.roll(values, amount, 1)


def shift(main, ext, step):
    rolled, rolled_ext = roll(main, -step), roll(ext, -step)
    edge = lane_ids(main.shape) == (LANES - 1 if step == 1 else 0)
    return jnp.where(edge, rolled_ext, rolled), jnp.where(edge, rolled, rolled_ext)


def row_up(values, size):
    return jnp.concatenate([values[size:], jnp.zeros((size, LANES), F32)], axis=0)


def row_down(values, size):
    return jnp.concatenate([jnp.zeros((size, LANES), F32), values[:-size]], axis=0)


def row_of_lane(shape):
    return ((lane_ids(shape) + 8) // 16) % 8


def pack(tiles):
    total = jnp.zeros(tiles[0].shape, F32)
    owner = row_of_lane(tiles[0].shape)
    for r in range(ROWS):
        total = jnp.where(owner == r, roll(tiles[r], 16 * r), total)
    return total


def load_tap(prod, t, group, size):
    rows = pl.ds(pl.multiple_of(t * NB + group * size, 8), size)
    main = prod[0:ROWS, rows, :].reshape(ROWS * size, LANES)
    return main, prod[ROWS, rows, :]


def combine(prod, group, size):
    mains, packs = [], []
    owner = row_of_lane((size, LANES))
    for q in (-1, 0, 1):
        up_main, up_pack = load_tap(prod, tap(1, q), group, size)
        mid_main, mid_pack = load_tap(prod, tap(0, q), group, size)
        down_main, down_pack = load_tap(prod, tap(-1, q), group, size)
        mains.append(mid_main + row_up(up_main, size) + row_down(down_main, size))
        packs.append(
            mid_pack
            + jnp.where(owner == ROWS - 1, 0.0, roll(up_pack, -16))
            + jnp.where(owner == 0, 0.0, roll(down_pack, 16))
        )
    lane = lane_ids(mains[1].shape)
    left_edge, right_edge = lane == 0, lane == LANES - 1

    def expand(values, q):
        return jnp.concatenate([roll(values, -16 * r - q) for r in range(ROWS)], axis=0)

    before, before_ext = roll(mains[0], 1), expand(packs[0], -1)
    after, after_ext = roll(mains[2], -1), expand(packs[2], 1)
    main = mains[1] + jnp.where(left_edge, before_ext, before) + jnp.where(right_edge, after_ext, after)
    ext = (
        expand(packs[1], 0)
        + jnp.where(left_edge, before, before_ext)
        + jnp.where(right_edge, after, after_ext)
    )
    return main, ext


def gelu_both(v):
    scale = math.sqrt(2.0 / math.pi)
    square = v * v
    t = jnp.tanh(scale * v * (1.0 + 0.044715 * square))
    half = 0.5 * (1.0 + t)
    slope = half + 0.5 * v * (1.0 - t * t) * (scale * (1.0 + 3.0 * 0.044715 * square))
    return v * half, slope


def rounded(values):
    return values.astype(BF16).astype(F32)


def resample_forward(prod, group, size, slopes, smooth):
    h, h_ext = combine(prod, group, size)
    h, h_ext = rounded(h), rounded(h_ext)
    hc, hc_ext = shift(h, h_ext, 1)
    acts = []
    for part, (x, y) in enumerate(((h, hc), (h_ext, hc_ext))):
        x_low, y_low = row_up(x, size), row_up(y, size)
        points = (x, (x + y) * 0.5, (x + x_low) * 0.5, (x + y + x_low + y_low) * 0.25)
        values = []
        for kind, point in enumerate(points):
            value, slope = gelu_both(point)
            values.append(value)
            slopes[part, kind, :, group_rows(group, size), :] = slope.reshape(ROWS, size, LANES)
        acts.append(values)
    left_even = shift(acts[0][1], acts[1][1], -1)
    left_odd = shift(acts[0][3], acts[1][3], -1)
    out = []
    for part in range(2):
        even = (left_even[part] + 2.0 * acts[part][0] + acts[part][1]) * 0.25
        odd = (left_odd[part] + 2.0 * acts[part][2] + acts[part][3]) * 0.25
        out.append(rounded((row_down(odd, size) + 2.0 * even + odd) * 0.25))
    main, ext = out
    store_shifted(smooth, shift(main, ext, -1)[0], main, shift(main, ext, 1)[0], group, size)


def group_rows(group, size):
    return pl.ds(pl.multiple_of(group * size, 8), size)


def store_shifted(ref, *args):
    before, here, after, group, size = args
    for q, values in enumerate((before, here, after)):
        ref[q, 1 : ROWS + 1, group_rows(group, size), :] = values.reshape(ROWS, size, LANES)


def resample_backward(prod, group, size, slopes, grads, packed):
    g, g_ext = combine(prod, group, size)
    g, g_ext = rounded(g), rounded(g_ext)
    gc, gc_ext = shift(g, g_ext, 1)
    base, moved = [], []
    for part, (x, y) in enumerate(((g, gc), (g_ext, gc_ext))):
        odd = (x + row_up(x, size)) * 0.25
        odd_next = (y + row_up(y, size)) * 0.25
        ups = (x * 0.25, (x + y) * 0.125, odd * 0.5, (odd + odd_next) * 0.25)
        b = [
            up * slopes[part, kind, :, group_rows(group, size), :].reshape(ROWS * size, LANES)
            for kind, up in enumerate(ups)
        ]
        half = b[1] * 0.5 + (b[3] + row_down(b[3], size)) * 0.25
        base.append(b[0] + (b[2] + row_down(b[2], size)) * 0.5 + half)
        moved.append(half)
    left, left_ext = shift(moved[0], moved[1], -1)
    main, ext = rounded(base[0] + left), rounded(base[1] + left_ext)
    store_shifted(grads, shift(main, ext, 1)[0], main, shift(main, ext, -1)[0], group, size)
    packed[group_rows(group, size), :] = pack([ext[r * size : (r + 1) * size] for r in range(ROWS)])


def products(weights, block, halo, prod):
    for r in range(0, ROWS, 2):
        pair = jnp.concatenate(
            [block[:, r].reshape(CH * NB, LANES), block[:, r + 1].reshape(CH * NB, LANES)], axis=1
        )
        out = jnp.dot(weights[...], pair, preferred_element_type=F32)
        prod[r] = out[:, :LANES]
        prod[r + 1] = out[:, LANES:]
    prod[ROWS] = jnp.dot(weights[...], halo.reshape(CH * NB, LANES), preferred_element_type=F32)


def row_pair(block, r):
    return jnp.concatenate(
        [block[:, r].reshape(CH * NB, LANES), block[:, r + 1].reshape(CH * NB, LANES)], axis=1
    )


def tap_rows(ref, r, sign):
    return jnp.concatenate(
        [ref[:, r + sign * p + 1].reshape(3 * NB, LANES) for p in (-1, 0, 1)], axis=0
    )


def tap_row_pair(ref, r, sign):
    return jnp.concatenate([tap_rows(ref, r, sign), tap_rows(ref, r + 1, sign)], axis=1)


def contract_last(a, b):
    return lax.dot_general(a, b, (((1,), (1,)), ((), ())), preferred_element_type=F32)


def kernel(
    field_ref, w1_ref, w2_ref, cot_ref, out_ref, grads_ref,
    rows32, w32, gath, gath_halo, edge, edge_in, cot32, lhs1, lhs2, wsend, wrecv,
    prod, slopes, shifted32, shifted, packed32, hgath,
    g2send, g2recv, part, part_in, rs_send, rs_recv, piece, sib_in,
    edge_sems, main_sems, halo_sems, w_sems, hg_sems, g2_sems, part_sems, rs_sems, ag_sems, sib_sems,
):
    chan = lax.axis_index("chan")
    space = lax.axis_index("space")
    core = lax.rem(space, 2)
    chip = lax.div(space, 2)
    left = lax.rem(space + SP - 1, SP)
    right = lax.rem(space + 1, SP)
    sibling = space + 1 - 2 * core
    scale = 1.0 / math.sqrt(ROWS * LANES * SP)

    def chan_at(k):
        return lax.rem(chan + k, CH)

    def peer_at(k):
        return lax.rem(chip + k, PEERS)

    def peer_space(k):
        return peer_at(k) * 2 + core

    barrier = pltpu.get_barrier_semaphore()

    def greet(axis, target):
        pl.semaphore_signal(barrier, inc=1, device_id={axis: target}, device_id_type=MESH)

    greet("space", left)
    greet("space", right)

    @pl.loop(1, CH)
    def _(k):
        greet("chan", chan_at(k))

    @pl.loop(1, PEERS)
    def _(k):
        greet("space", peer_space(k))

    def remote(src, dst, sems, k, axis, target):
        return pltpu.make_async_remote_copy(
            src_ref=src, dst_ref=dst, send_sem=sems.at[0, k], recv_sem=sems.at[1, k],
            device_id={axis: target}, device_id_type=MESH,
        )

    for which, ref in enumerate((field_ref, cot_ref)):
        rows32[...] = ref[...].astype(F32).reshape(NB * ROWS, LANES)
        tiles = [rows32[pl.ds(r, NB, stride=ROWS), :] for r in range(ROWS)]
        for r in range(ROWS):
            gath[which, chan, r] = tiles[r].astype(BF16)
            if which == 1:
                cot32[r] = tiles[r]
        edge[which] = pack(tiles).astype(BF16)

    pl.semaphore_wait(barrier, CH - 1 + PEERS - 1 + 2)

    to_left = remote(edge, edge_in.at[0], edge_sems, 0, "space", left)
    to_right = remote(edge, edge_in.at[1], edge_sems, 1, "space", right)
    to_left.start()
    to_right.start()

    def main_copy(which, k, slot):
        return remote(
            gath.at[which, slot], gath.at[which, slot], main_sems.at[which], k, "chan", chan_at(k)
        )

    def halo_copy(k, slot):
        return remote(gath_halo.at[slot], gath_halo.at[slot], halo_sems, k, "chan", chan_at(k))

    for which in range(2):
        @pl.loop(1, CH)
        def _(k):
            main_copy(which, k, chan).start()

    for which, ref in enumerate((w1_ref, w2_ref)):
        w32[:, 0:9, :] = ref[...].astype(F32)
        if which == 0:
            for t in range(9):
                lhs1[t * NB : (t + 1) * NB, :] = w32[:, t, :].astype(BF16)
        lane = lane_ids((NB, LANES))
        for k in range(3):
            taps = range(4 * k, min(4 * k + 4, 9))
            loaded = [w32[:, 8 - t, :] for t in taps]
            for dest in range(CH):
                half, place = dest // 4, dest % 4
                total = jnp.zeros((NB, LANES), F32)
                for t, values in zip(taps, loaded):
                    source = values[:, half * LANES : (half + 1) * LANES]
                    total = jnp.where(
                        lane // NB == t % 4, roll(source, (t % 4 - place) * NB), total
                    )
                wsend[dest, which, k] = total.astype(BF16)

    def w_copy(k, dest, slot):
        return remote(wsend.at[dest], wrecv.at[slot], w_sems, k, "chan", chan_at(k))

    @pl.loop(1, CH)
    def _(k):
        w_copy(k, chan_at(k), chan).start()

    wrecv[chan] = wsend[chan]

    to_left.wait_recv()
    to_right.wait_recv()
    for which in range(2):
        from_right = edge_in[0, which].astype(F32)
        from_left = edge_in[1, which].astype(F32)
        merged = jnp.where(lane_ids((NB, LANES)) % 16 < 8, from_right, from_left)
        gath_halo[chan, which] = merged.astype(BF16)

    @pl.loop(1, CH)
    def _(k):
        halo_copy(k, chan).start()

    @pl.loop(1, CH)
    def _(k):
        main_copy(0, k, chan_at(CH - k)).wait_recv()
        halo_copy(k, chan_at(CH - k)).wait_recv()

    group_size = 8
    shifted32[:, 0] = jnp.zeros((3, NB, LANES), F32)
    shifted32[:, ROWS + 1] = jnp.zeros((3, NB, LANES), F32)
    products(lhs1, gath.at[0], gath_halo[:, 0], prod)

    @pl.loop(0, NB // group_size)
    def _(group):
        resample_forward(prod, group, group_size, slopes, shifted32)

    shifted[0] = shifted32[...].astype(BF16)

    @pl.loop(1, CH)
    def _(k):
        main_copy(1, k, chan_at(CH - k)).wait_recv()
        w_copy(k, chan_at(k), chan_at(CH - k)).wait_recv()

    for which in range(2):
        for k in range(3):
            turned = wrecv[:, which, k].reshape(CH * NB, LANES).T
            if k < 2:
                lhs2[which, k * LANES : (k + 1) * LANES, :] = turned
            else:
                lhs2[which, 2 * LANES :, :] = turned[:NB]
    products(lhs2.at[1], gath.at[1], gath_halo[:, 1], prod)

    @pl.loop(0, NB // group_size)
    def _(group):
        resample_backward(prod, group, group_size, slopes, shifted32, packed32)

    shifted[1] = shifted32[...].astype(BF16)
    hgath[chan, 0:ROWS] = shifted[1, 1, 1 : ROWS + 1]
    hgath[chan, ROWS] = packed32[...].astype(BF16)

    def hg_copy(k, slot):
        return remote(hgath.at[slot], hgath.at[slot], hg_sems, k, "chan", chan_at(k))

    @pl.loop(1, CH)
    def _(k):
        hg_copy(k, chan).start()

    total = jnp.zeros((CH * NB, 3 * LANES), F32)
    for r in range(0, ROWS, 2):
        rhs = tap_row_pair(shifted.at[0], r, 1)
        rhs = jnp.concatenate([rhs, jnp.zeros((3 * NB, 2 * LANES), BF16)], axis=0)
        total = total + contract_last(row_pair(gath.at[1], r), rhs)
    total = (total * scale).astype(BF16)
    for k in range(3):
        g2send[:, k] = total[:, k * LANES : (k + 1) * LANES].reshape(CH, NB, LANES)

    def g2_copy(k, dest, slot):
        return remote(g2send.at[dest], g2recv.at[slot], g2_sems, k, "chan", chan_at(k))

    @pl.loop(1, CH)
    def _(k):
        g2_copy(k, chan_at(k), chan).start()

    g2recv[chan] = g2send[chan]

    total = jnp.zeros((9 * NB, CH * NB), F32)
    for r in range(0, ROWS, 2):
        total = total + contract_last(
            tap_row_pair(shifted.at[1], r, -1), row_pair(gath.at[0], r)
        )
    part[0] = total * scale

    @pl.loop(1, CH)
    def _(k):
        g2_copy(k, chan_at(k), chan_at(CH - k)).wait_recv()

    lane = lane_ids((NB, LANES))
    for k in range(3):
        loaded = [g2recv[s, k].astype(F32) for s in range(CH)]
        for t in range(4 * k, min(4 * k + 4, 9)):
            for half in range(2):
                total = jnp.zeros((NB, LANES), F32)
                for place in range(4):
                    moved = roll(loaded[4 * half + place], (place - t % 4) * NB)
                    total = jnp.where(lane // NB == place, moved, total)
                part[1, t * NB : (t + 1) * NB, half * LANES : (half + 1) * LANES] = total

    swap = remote(part.at[1 - core], part_in, part_sems, 0, "space", sibling)
    swap.start()
    swap.wait_recv()
    for tile in range(0, 36, 2):
        rows = tile // 2 * 16
        both = part[core, rows : rows + 16, :] + part_in[rows : rows + 16, :]
        for half in range(2):
            rs_send[(tile + half) // TILES, (tile + half) % TILES] = both[
                :, half * LANES : (half + 1) * LANES
            ].astype(BF16)
    rs_send[12:] = jnp.zeros((4, TILES, 16, LANES), BF16)

    def rs_copy(k, dest, slot):
        return remote(rs_send.at[dest], rs_recv.at[slot], rs_sems, k, "space", peer_space(k))

    @pl.loop(1, PEERS)
    def _(k):
        rs_copy(k, peer_at(k), chip).start()

    rs_recv[chip] = rs_send[chip]

    @pl.loop(1, CH)
    def _(k):
        hg_copy(k, chan_at(CH - k)).wait_recv()

    products(lhs2.at[0], hgath, hgath[:, ROWS], prod)

    @pl.loop(0, NB // group_size)
    def _(group):
        main, _ = combine(prod, group, group_size)
        rows = group_rows(group, group_size)
        cot32[:, rows, :] = cot32[:, rows, :] + main.reshape(ROWS, group_size, LANES)

    out_ref[...] = cot32[...].astype(BF16)

    @pl.loop(1, PEERS)
    def _(k):
        rs_copy(k, peer_at(k), peer_at(PEERS - k)).wait_recv()

    total = rs_recv[0].astype(F32)
    for s in range(1, PEERS):
        total = total + rs_recv[s].astype(F32)
    piece[chip] = total.astype(BF16)

    def ag_copy(k, slot):
        return remote(piece.at[slot], piece.at[slot], ag_sems, k, "space", peer_space(k))

    def sib_copy(k, slot):
        return remote(piece.at[slot], sib_in.at[slot], sib_sems, k, "space", sibling)

    @pl.loop(1, PEERS)
    def _(k):
        ag_copy(k, chip).start()

    sib_copy(0, chip).start()

    @pl.loop(1, PEERS)
    def _(k):
        ag_copy(k, peer_at(PEERS - k)).wait_recv()
        sib_copy(k, peer_at(PEERS - k)).start()

    @pl.loop(0, PEERS)
    def _(k):
        sib_copy(k, peer_at(PEERS - k)).wait_recv()

    for tile in range(36):
        rows = slice(tile // 2 * 16, tile // 2 * 16 + 16)
        lanes = slice(tile % 2 * LANES, (tile % 2 + 1) * LANES)
        grads_ref[core, rows, lanes] = piece[tile // TILES, tile % TILES]
        grads_ref[1 - core, rows, lanes] = sib_in[tile // TILES, tile % TILES]

    to_left.wait_send()
    to_right.wait_send()
    swap.wait_send()
    sib_copy(0, chip).wait_send()

    @pl.loop(1, CH)
    def _(k):
        main_copy(0, k, chan).wait_send()
        main_copy(1, k, chan).wait_send()
        halo_copy(k, chan).wait_send()
        w_copy(k, chan_at(k), chan).wait_send()
        hg_copy(k, chan).wait_send()
        g2_copy(k, chan_at(k), chan).wait_send()

    @pl.loop(1, PEERS)
    def _(k):
        rs_copy(k, peer_at(k), chip).wait_send()
        ag_copy(k, chip).wait_send()
        sib_copy(k, peer_at(PEERS - k)).wait_send()


def on_device(field, first_weight, second_weight, cotangent):
    vmem = pl.BlockSpec(memory_space=pltpu.VMEM)
    dma = pltpu.SemaphoreType.DMA
    out, grads = pl.pallas_call(
        kernel,
        out_shape=(
            jax.ShapeDtypeStruct((ROWS, NB, LANES), BF16),
            jax.ShapeDtypeStruct((2, 9 * NB, CH * NB), BF16),
        ),
        in_specs=[vmem] * 4,
        out_specs=(vmem, vmem),
        scratch_shapes=[
            pltpu.VMEM((NB * ROWS, LANES), F32),
            pltpu.VMEM((NB, 16, CH * NB), F32),
            pltpu.VMEM((2, CH, ROWS, NB, LANES), BF16),
            pltpu.VMEM((CH, 2, NB, LANES), BF16),
            pltpu.VMEM((2, NB, LANES), BF16),
            pltpu.VMEM((2, 2, NB, LANES), BF16),
            pltpu.VMEM((ROWS, NB, LANES), F32),
            pltpu.VMEM((9 * NB, CH * NB), BF16),
            pltpu.VMEM((2, 9 * NB, CH * NB), BF16),
            pltpu.VMEM((CH, 2, 3, NB, LANES), BF16),
            pltpu.VMEM((CH, 2, 3, NB, LANES), BF16),
            pltpu.VMEM((ROWS + 1, 9 * NB, LANES), F32),
            pltpu.VMEM((2, 4, ROWS, NB, LANES), F32),
            pltpu.VMEM((3, ROWS + 2, NB, LANES), F32),
            pltpu.VMEM((2, 3, ROWS + 2, NB, LANES), BF16),
            pltpu.VMEM((NB, LANES), F32),
            pltpu.VMEM((CH, ROWS + 1, NB, LANES), BF16),
            pltpu.VMEM((CH, 3, NB, LANES), BF16),
            pltpu.VMEM((CH, 3, NB, LANES), BF16),
            pltpu.VMEM((2, 9 * NB, CH * NB), F32),
            pltpu.VMEM((9 * NB, CH * NB), F32),
            pltpu.VMEM((PEERS, TILES, 16, LANES), BF16),
            pltpu.VMEM((PEERS, TILES, 16, LANES), BF16),
            pltpu.VMEM((PEERS, TILES, 16, LANES), BF16),
            pltpu.VMEM((PEERS, TILES, 16, LANES), BF16),
            dma((2, 2)),
            dma((2, 2, CH)),
            dma((2, CH)),
            dma((2, CH)),
            dma((2, CH)),
            dma((2, CH)),
            dma((2, 1)),
            dma((2, PEERS)),
            dma((2, PEERS)),
            dma((2, PEERS)),
        ],
        compiler_params=pltpu.CompilerParams(
            collective_id=0, has_side_effects=True, vmem_limit_bytes=40 * 1024 * 1024
        ),
    )(field, first_weight, second_weight, cotangent)
    field_grad = out.transpose(1, 0, 2)
    grads = grads.astype(F32).reshape(2, 9, NB, CH * NB).transpose(0, 2, 1, 3)
    return (field_grad, grads[0], grads[1])


def solution(mesh):
    in_specs = (
        P("chan", None, "space"),
        P("chan", None, None),
        P("chan", None, None),
        P("chan", None, "space"),
    )
    out_specs = (P("chan", None, "space"), P("chan", None, None), P("chan", None, None))
    return jax.shard_map(
        on_device, mesh=mesh, in_specs=in_specs, out_specs=out_specs, check_vma=False
    )
```

time: 503 us -> 69.7 us (0.14)
  waiting for transfers between devices: 358 us -> 0 us
  Pallas kernels: 0 us -> 65.4 us
  blocking collectives: 54.4 us -> 0 us
  starting transfers between devices: 37.2 us -> 0 us
  matrix products: 18.6 us -> 0 us
  between operations: 14.2 us -> 0.69 us
  local copies, waits for them, and re-layouts: 12.9 us -> 3.4 us
  other arithmetic: 6.88 us -> 0.05 us
    psum x1 -> x0, waiting for transfers between devices: 280 us -> none  [on_device(): first_grad, second_grad = lax.psum((first_grad, second_grad), 'space')]
    reduce_scatter x2 -> x0, waiting for transfers between devices: 73.8 us -> none  [reduce_back(): lax.psum_scatter(conv_back(padded, weight), 'chan', scatter_dimension=0,...]
    pallas_call x0 -> x1, Pallas kernels: none -> 65.4 us  [on_device(): pl.pallas_call(kernel, out_shape=(jax.ShapeDtypeStruct((ROWS, NB, LANES),...]
    all_gather x2 -> x0, blocking collectives: 54.4 us -> none  [collect(): return lax.all_gather(values, 'chan', axis=0, tiled=True)]
    ppermute x12 -> x0, starting transfers between devices: 37.1 us -> none  [the longest x6 24.7 us: with_halo(): lax.ppermute(lax.slice_in_dim(block, 0, width, axis=dim), axis, backward)]
    dot_general x45 -> x0, matrix products: 18.6 us -> none  [the longest x18 8.12 us: conv_back(): jnp.einsum('oi,orc->irc', weight[:, 3 * tap_row + tap_col, :], window, pr...]
    unnamed x15 -> x9, local copies, waits for them, and re-layouts: 8.12 us -> 2.55 us
  transfers between devices with their start and end apart: 15 -> 0, of which waited for: 7 -> 0; matrix products, arithmetic and copies ran while one was open for 3% -> 0% of each run, Pallas kernels for 0% -> 0%
where the time goes in v1:
time: 69.7 us; the launch traced here: 69.5 us
  Pallas kernels  65.4 us (94%)
  local copies, waits for them, and re-layouts  3.4 us (5%)
    pallas_call x1, Pallas kernels, on_device(): pl.pallas_call(kernel, out_shape=(jax.ShapeDtypeStruct((ROWS, NB, LANES),...  65.4 us
    unnamed x9, local copies, waits for them, and re-layouts  2.55 us

profile of v1, /device:TPU:1, one launch (start us, length us, event | category | flops | bytes accessed | tf_op | source)
XLA Modules:
  0.0 69.5 jit_solution(665045036839128756)
XLA Ops:
  0.6 0.0 copy-start.2
  0.6 1.0 %copy.7.w1_ref = bf16[32,9,256]{2,1,0:T(8,128)(2,1)S(1)} copy(bf16[32,9,256]{2,0,1:T(8,128)(2,1)} %param.5) | data formatting | bytes 294912 | tf_op args[1]
  1.7 0.0 copy-done.2
  1.7 0.0 copy-start
  1.7 0.0 copy-start.1
  1.7 0.1 copy.8.w2_ref
  1.8 0.7 %copy-done = bf16[32,8,128]{2,1,0:T(8,128)(2,1)S(1)} copy-done((bf16[32,8,128]{2,1,0:T(8,128)(2,1)S(1)}, bf16[32,8,128]{2,1,0:T(8,128)(2,1)}, u32[]{:S(2)}) %copy-start) | copy-done | bytes 65560
  2.5 0.0 copy-done.1
  2.6 65.4 %shard_map.67 = (bf16[8,32,128]{2,1,0:T(8,128)(2,1)S(1)}, bf16[2,288,256]{2,1,0:T(8,128)(2,1)S(1)}) custom-call(bf16[32,8,128]{2,1,0:T(8,128)(2,1)S(1)} %copy-done, bf16[32,9,256]{2,1,0:T(8,128)(2,1)S(1)} %copy.7.w1_ref, bf16[32,9,256]{2,1,0:T(8,128)(2,1)S(1)} %copy.8.w2_ref, bf16[32,8,128]{2,1,0:T(8,128)(2,1)S(1)} %copy-done.1), custom_call_target="tpu_custom_call" | custom-call | tf_op jit(solution)/shard_map/pallas_call | solution.py:497
  68.0 0.7 copy.9
  68.7 0.9 %slice_bitcast_fusion = (f32[32,9,256]{2,0,1:T(8,128)}, f32[32,9,256]{2,0,1:T(8,128)}) fusion(f32[2,32,9,256]{3,1,2,0:T(8,128)S(1)} %convert_bitcast_fusion), kind=kLoop, calls=%fused_computation.1 | loop fusion | bytes 1179648 | tf_op jit(solution)/shard_map/squeeze | solution.py:548
  (1 shorter events, 0.0 us)
Async XLA Ops:
  0.6 1.0 %copy-start.2 = (bf16[32,9,256]{2,0,1:T(8,128)(2,1)S(1)}, bf16[32,9,256]{2,0,1:T(8,128)(2,1)}, u32[]{:S(2)}) copy-start(bf16[32,9,256]{2,0,1:T(8,128)(2,1)} %param.6) | copy-start | bytes 442372
  1.7 0.8 %copy-start = (bf16[32,8,128]{2,1,0:T(8,128)(2,1)S(1)}, bf16[32,8,128]{2,1,0:T(8,128)(2,1)}, u32[]{:S(2)}) copy-start(bf16[32,8,128]{2,1,0:T(8,128)(2,1)} %field_ref.1) | copy-start | bytes 196612
  1.7 0.9 %copy-start.1 = (bf16[32,8,128]{2,1,0:T(8,128)(2,1)S(1)}, bf16[32,8,128]{2,1,0:T(8,128)(2,1)}, u32[]{:S(2)}) copy-start(bf16[32,8,128]{2,1,0:T(8,128)(2,1)} %cot_ref.1) | copy-start | bytes 196612

commit v2 on v1

v2 whole, which is shorter than its diff:
```python
import math

import jax
import jax.numpy as jnp
from jax import lax
from jax.experimental import pallas as pl
from jax.experimental.pallas import tpu as pltpu
from jax.sharding import PartitionSpec as P

MESH = pl.DeviceIdType.MESH
F32 = jnp.float32
BF16 = jnp.bfloat16
CH = 8
SP = 32
NB = 32
ROWS = 8
LANES = 128
PEERS = SP // 2
OWNERS = 12
TILES = 3
TAPS = [(p, q) for p in (-1, 0, 1) for q in (-1, 0, 1)]


def tap(p, q):
    return 3 * (p + 1) + q + 1


def lane_ids(shape):
    return lax.broadcasted_iota(jnp.int32, shape, len(shape) - 1)


def roll(values, amount):
    amount = amount % LANES
    if amount == 0:
        return values
    return pltpu.roll(values, amount, 1)


def shift(main, ext, step):
    rolled, rolled_ext = roll(main, -step), roll(ext, -step)
    edge = lane_ids(main.shape) == (LANES - 1 if step == 1 else 0)
    return jnp.where(edge, rolled_ext, rolled), jnp.where(edge, rolled, rolled_ext)


def row_up(values, size):
    return jnp.concatenate([values[size:], jnp.zeros((size, LANES), F32)], axis=0)


def row_down(values, size):
    return jnp.concatenate([jnp.zeros((size, LANES), F32), values[:-size]], axis=0)


def row_of_lane(shape, offset=0):
    return ((lane_ids(shape) + 8 - offset) // 16) % 8


def pack(tiles):
    total = jnp.zeros(tiles[0].shape, F32)
    owner = row_of_lane(tiles[0].shape)
    for r in range(ROWS):
        total = jnp.where(owner == r, roll(tiles[r], 16 * r), total)
    return total


def load_tap(prod, t, group, size):
    rows = pl.ds(pl.multiple_of(t * NB + group * size, 8), size)
    main = prod[0:ROWS, rows, :].reshape(ROWS * size, LANES)
    return main, prod[ROWS, rows, :]


def combine(prod, group, size, offset=0):
    mains, packs = [], []
    owner = row_of_lane((size, LANES), offset)
    for q in (-1, 0, 1):
        up_main, up_pack = load_tap(prod, tap(1, q), group, size)
        mid_main, mid_pack = load_tap(prod, tap(0, q), group, size)
        down_main, down_pack = load_tap(prod, tap(-1, q), group, size)
        mains.append(mid_main + row_up(up_main, size) + row_down(down_main, size))
        packs.append(
            mid_pack
            + jnp.where(owner == ROWS - 1, 0.0, roll(up_pack, -16))
            + jnp.where(owner == 0, 0.0, roll(down_pack, 16))
        )
    lane = lane_ids(mains[1].shape)
    left_edge, right_edge = lane == 0, lane == LANES - 1

    def expand(values, q):
        return jnp.concatenate([roll(values, -16 * r - q - offset) for r in range(ROWS)], axis=0)

    before, before_ext = roll(mains[0], 1), expand(packs[0], -1)
    after, after_ext = roll(mains[2], -1), expand(packs[2], 1)
    main = mains[1] + jnp.where(left_edge, before_ext, before) + jnp.where(right_edge, after_ext, after)
    ext = (
        expand(packs[1], 0)
        + jnp.where(left_edge, before, before_ext)
        + jnp.where(right_edge, after, after_ext)
    )
    return main, ext


def gelu_both(v):
    scale = math.sqrt(2.0 / math.pi)
    square = v * v
    t = jnp.tanh(scale * v * (1.0 + 0.044715 * square))
    half = 0.5 * (1.0 + t)
    slope = half + 0.5 * v * (1.0 - t * t) * (scale * (1.0 + 3.0 * 0.044715 * square))
    return v * half, slope


def rounded(values):
    return values.astype(BF16).astype(F32)


def resample_forward(prod, group, size, slopes, smooth):
    h, h_ext = combine(prod, group, size)
    h, h_ext = rounded(h), rounded(h_ext)
    hc, hc_ext = shift(h, h_ext, 1)
    acts = []
    for part, (x, y) in enumerate(((h, hc), (h_ext, hc_ext))):
        x_low, y_low = row_up(x, size), row_up(y, size)
        points = (x, (x + y) * 0.5, (x + x_low) * 0.5, (x + y + x_low + y_low) * 0.25)
        values = []
        for kind, point in enumerate(points):
            value, slope = gelu_both(point)
            values.append(value)
            slopes[part, kind, :, group_rows(group, size), :] = slope.reshape(ROWS, size, LANES)
        acts.append(values)
    left_even = shift(acts[0][1], acts[1][1], -1)
    left_odd = shift(acts[0][3], acts[1][3], -1)
    out = []
    for part in range(2):
        even = (left_even[part] + 2.0 * acts[part][0] + acts[part][1]) * 0.25
        odd = (left_odd[part] + 2.0 * acts[part][2] + acts[part][3]) * 0.25
        out.append(rounded((row_down(odd, size) + 2.0 * even + odd) * 0.25))
    main, ext = out
    store_shifted(smooth, shift(main, ext, -1)[0], main, shift(main, ext, 1)[0], group, size)


def group_rows(group, size):
    return pl.ds(pl.multiple_of(group * size, 8), size)


def store_shifted(ref, *args):
    before, here, after, group, size = args
    for q, values in enumerate((before, here, after)):
        ref[q, 1 : ROWS + 1, group_rows(group, size), :] = values.reshape(ROWS, size, LANES)


def resample_backward(prod, group, size, slopes, grads, packed):
    g, g_ext = combine(prod, group, size, 8)
    g, g_ext = rounded(g), rounded(g_ext)
    gc, gc_ext = shift(g, g_ext, 1)
    base, moved = [], []
    for part, (x, y) in enumerate(((g, gc), (g_ext, gc_ext))):
        odd = (x + row_up(x, size)) * 0.25
        odd_next = (y + row_up(y, size)) * 0.25
        ups = (x * 0.25, (x + y) * 0.125, odd * 0.5, (odd + odd_next) * 0.25)
        b = [
            up * slopes[part, kind, :, group_rows(group, size), :].reshape(ROWS * size, LANES)
            for kind, up in enumerate(ups)
        ]
        half = b[1] * 0.5 + (b[3] + row_down(b[3], size)) * 0.25
        base.append(b[0] + (b[2] + row_down(b[2], size)) * 0.5 + half)
        moved.append(half)
    left, left_ext = shift(moved[0], moved[1], -1)
    main, ext = rounded(base[0] + left), rounded(base[1] + left_ext)
    store_shifted(grads, shift(main, ext, 1)[0], main, shift(main, ext, -1)[0], group, size)
    packed[group_rows(group, size), :] = pack([ext[r * size : (r + 1) * size] for r in range(ROWS)])


def products(weights, block, halo, prod):
    for r in range(0, ROWS, 2):
        pair = jnp.concatenate(
            [block[:, r].reshape(CH * NB, LANES), block[:, r + 1].reshape(CH * NB, LANES)], axis=1
        )
        out = jnp.dot(weights, pair, preferred_element_type=F32)
        prod[r] = out[:, :LANES]
        prod[r + 1] = out[:, LANES:]
    prod[ROWS] = jnp.dot(weights, halo.reshape(CH * NB, LANES), preferred_element_type=F32)


def row_pair(block, r):
    return jnp.concatenate(
        [block[:, r].reshape(CH * NB, LANES), block[:, r + 1].reshape(CH * NB, LANES)], axis=1
    )


def tap_rows(ref, r, sign):
    return jnp.concatenate(
        [ref[:, r + sign * p + 1].reshape(3 * NB, LANES) for p in (-1, 0, 1)], axis=0
    )


def tap_row_pair(ref, r, sign):
    return jnp.concatenate([tap_rows(ref, r, sign), tap_rows(ref, r + 1, sign)], axis=1)


def contract_last(a, b):
    return lax.dot_general(a, b, (((1,), (1,)), ((), ())), preferred_element_type=F32)


HOPS = (
    ((0, 0), (1, 0), (-1, 0)),
    ((0, 0), (-1, 0), (1, 0)),
    ((0, 0), (0, 1), (0, 1)),
    ((0, 0), (2, 0), (2, 0)),
    ((0, 1), (1, 0), (-1, 1)),
    ((0, 1), (-1, 0), (1, 1)),
    ((2, 0), (0, 1), (2, 1)),
)


def kernel(
    field_hbm, w1_hbm, w2_hbm, cot_hbm, out_ref, grads_ref,
    field_in, cot_in, w1_in, w_in,
    rows32, gath, halo, edge, edge_in, cot32, lhs2, wsend, wrecv,
    prod, slopes, shifted32, shifted, packed32, hgath,
    g2part, g2swap, g2send, g2recv, g1part, g1swap, rs_send, rs_recv, piece, sib_in,
    in_sems, edge_sems, main_sems, halo_sems, w_sems, wsib_sems, hg_sems, g2swap_sems, g2_sems,
    g1_sems, rs_sems, ag_sems, sib_sems,
):
    chan = lax.axis_index("chan")
    space = lax.axis_index("space")
    core = lax.rem(space, 2)
    chip = lax.div(space, 2)
    line, level = lax.div(chan, 2), lax.rem(chan, 2)
    left = lax.rem(space + SP - 1, SP)
    right = lax.rem(space + 1, SP)
    sibling = space + 1 - 2 * core
    scale = 1.0 / math.sqrt(ROWS * LANES * SP)

    def chan_at(k):
        return lax.rem(chan + k, CH)

    def block_at(place):
        step, other = place
        at = 1 - level if other else level
        return lax.rem(line + step + 4, 4) * 2 + at

    barrier = pltpu.get_barrier_semaphore()

    def greet(**target):
        pl.semaphore_signal(barrier, inc=1, device_id=target, device_id_type=MESH)

    greet(space=left)
    greet(space=right)

    @pl.loop(1, CH)
    def _(k):
        greet(chan=chan_at(k))
        greet(chan=chan_at(k), space=sibling)

    @pl.loop(1, PEERS)
    def _(k):
        greet(space=lax.rem(chip + k, PEERS) * 2 + core)

    def fetch(src, dst, k):
        return pltpu.make_async_copy(src, dst, in_sems.at[k])

    fetch(field_hbm, field_in, 0).start()
    fetch(cot_hbm, cot_in, 1).start()
    fetch(w1_hbm, w1_in, 2).start()

    @pl.when(core == 0)
    def _():
        fetch(w1_hbm, w_in, 3).start()

    @pl.when(core == 1)
    def _():
        fetch(w2_hbm, w_in, 3).start()

    def remote(src, dst, sems, k, **target):
        return pltpu.make_async_remote_copy(
            src_ref=src, dst_ref=dst, send_sem=sems.at[0, k], recv_sem=sems.at[1, k],
            device_id=target, device_id_type=MESH,
        )

    def hop(buf, sems, j):
        sent = block_at(HOPS[j][0])
        return remote(buf.at[sent], buf.at[sent], sems, j, chan=block_at(HOPS[j][1]))

    def hop_in(buf, sems, j):
        got = block_at(HOPS[j][2])
        return remote(buf.at[got], buf.at[got], sems, j, chan=block_at(HOPS[j][1]))

    def first_hops(buf, sems):
        for j in range(4):
            hop(buf, sems, j).start()

    def second_hops(buf, sems):
        hop_in(buf, sems, 2).wait_recv()
        hop(buf, sems, 4).start()
        hop(buf, sems, 5).start()
        hop_in(buf, sems, 3).wait_recv()
        hop(buf, sems, 6).start()

    def last_hops(buf, sems):
        for j in (0, 1, 4, 5, 6):
            hop_in(buf, sems, j).wait_recv()

    def split_rows(source):
        rows32[...] = source[...].astype(F32).reshape(NB * ROWS, LANES)
        return [rows32[pl.ds(r, NB, stride=ROWS), :] for r in range(ROWS)]

    fetch(field_hbm, field_in, 0).wait()
    field_rows = split_rows(field_in)
    for r in range(ROWS):
        gath[0, chan, r] = field_rows[r].astype(BF16)

    pl.semaphore_wait(barrier, 2 * (CH - 1) + PEERS - 1 + 2)
    first_hops(gath.at[0], main_sems.at[0])

    fetch(cot_hbm, cot_in, 1).wait()
    edge_field = pack(field_rows)
    cot_rows = split_rows(cot_in)
    for r in range(ROWS):
        gath[1, chan, r] = cot_rows[r].astype(BF16)
        cot32[r] = cot_rows[r]
    lane = lane_ids((NB, LANES))
    near = (lane % 16 < 4) | (lane % 16 >= 12)
    edge[...] = jnp.where(near, edge_field, roll(pack(cot_rows), 8)).astype(BF16)
    to_left = remote(edge, edge_in.at[0], edge_sems, 0, space=left)
    to_right = remote(edge, edge_in.at[1], edge_sems, 1, space=right)
    to_left.start()
    to_right.start()
    first_hops(gath.at[1], main_sems.at[1])

    fetch(w1_hbm, w1_in, 2).wait()
    fetch(w1_hbm, w_in, 3).wait()
    for k in range(3):
        taps = range(4 * k, min(4 * k + 4, 9))
        loaded = [w_in[8 - t].astype(F32) for t in taps]
        for dest in range(CH):
            half, place = dest // 4, dest % 4
            total = jnp.zeros((NB, LANES), F32)
            for t, values in zip(taps, loaded):
                source = values[:, half * LANES : (half + 1) * LANES]
                total = jnp.where(lane // NB == t % 4, roll(source, (t % 4 - place) * NB), total)
            wsend[dest, k] = total.astype(BF16)

    def w_copy(k, dest, slot):
        return remote(wsend.at[dest], wrecv.at[core, slot], w_sems, k, chan=chan_at(k))

    @pl.loop(1, CH)
    def _(k):
        w_copy(k, chan_at(k), chan).start()

    wrecv[core, chan] = wsend[chan]

    to_left.wait_recv()
    to_right.wait_recv()
    from_right = edge_in[0].astype(F32)
    from_left = edge_in[1].astype(F32)
    halo[chan] = jnp.where(lane % 8 < 4, from_right, from_left).astype(BF16)

    def halo_copy(k, slot):
        return remote(halo.at[slot], halo.at[slot], halo_sems, k, chan=chan_at(k))

    @pl.loop(1, CH)
    def _(k):
        halo_copy(k, chan).start()

    second_hops(gath.at[0], main_sems.at[0])
    second_hops(gath.at[1], main_sems.at[1])

    last_hops(gath.at[0], main_sems.at[0])

    @pl.loop(1, CH)
    def _(k):
        halo_copy(k, chan_at(CH - k)).wait_recv()

    group_size = 8
    shifted32[:, 0] = jnp.zeros((3, NB, LANES), F32)
    shifted32[:, ROWS + 1] = jnp.zeros((3, NB, LANES), F32)
    products(w1_in[...].reshape(9 * NB, CH * NB), gath.at[0], halo[...], prod)

    @pl.loop(0, NB // group_size)
    def _(group):
        resample_forward(prod, group, group_size, slopes, shifted32)

    shifted[0] = shifted32[...].astype(BF16)

    @pl.loop(1, CH)
    def _(k):
        w_copy(k, chan_at(k), chan_at(CH - k)).wait_recv()

    w_out = remote(wrecv.at[core], wrecv.at[core], wsib_sems, 0, space=sibling)
    w_out.start()

    last_hops(gath.at[1], main_sems.at[1])
    total = jnp.zeros((CH * NB, 3 * LANES), F32)
    for r in range(0, ROWS, 2):
        rhs = tap_row_pair(shifted.at[0], r, 1)
        rhs = jnp.concatenate([rhs, jnp.zeros((3 * NB, 2 * LANES), BF16)], axis=0)
        total = total + contract_last(row_pair(gath.at[1], r), rhs)
    total = total * scale
    for k in range(3):
        g2part[:, k] = total[:, k * LANES : (k + 1) * LANES].reshape(CH, NB, LANES)

    g2_swap = remote(g2part.at[pl.ds(4 - 4 * core, 4)], g2swap, g2swap_sems, 0, space=sibling)
    g2_swap.start()

    remote(wrecv.at[1 - core], wrecv.at[1 - core], wsib_sems, 0, space=sibling).wait_recv()

    def turn_weights(which):
        for k in range(3):
            turned = wrecv[which, :, k].reshape(CH * NB, LANES).T
            if k < 2:
                lhs2[which, k * LANES : (k + 1) * LANES, :] = turned
            else:
                lhs2[which, 2 * LANES :, :] = turned[:NB]

    turn_weights(1)
    products(lhs2[1], gath.at[1], halo[...], prod)

    def g2_copy(j, slot):
        return remote(
            g2send.at[j], g2recv.at[slot], g2_sems, slot, chan=core * 4 + j, space=2 * chip + 1
        )

    def g2_sent(j):
        return pltpu.make_async_remote_copy(
            src_ref=g2send.at[j], dst_ref=g2recv.at[chan], send_sem=g2_sems.at[0, j],
            recv_sem=g2_sems.at[1, chan],
            device_id={"chan": core * 4 + j, "space": 2 * chip + 1}, device_id_type=MESH,
        )

    g2_swap.wait_recv()
    for j in range(4):
        g2send[j] = (g2part[core * 4 + j] + g2swap[j]).astype(BF16)
        mine = (core == 1) & (core * 4 + j == chan)

        @pl.when(mine)
        def _():
            g2recv[chan] = g2send[j]

        @pl.when(jnp.logical_not(mine))
        def _():
            g2_sent(j).start()

    @pl.loop(0, NB // group_size)
    def _(group):
        resample_backward(prod, group, group_size, slopes, shifted32, packed32)

    shifted[1] = shifted32[...].astype(BF16)
    hgath[chan, 0:ROWS] = shifted[1, 1, 1 : ROWS + 1]
    hgath[chan, ROWS] = packed32[...].astype(BF16)
    first_hops(hgath, hg_sems)

    def g1_copy(p):
        return remote(g1part.at[p], g1swap.at[p], g1_sems, p, space=sibling)

    for p in range(3):
        total = jnp.zeros((3 * NB, CH * NB), F32)
        for r in range(0, ROWS, 2):
            lhs = jnp.concatenate(
                [shifted[1, :, r + i - p + 2].reshape(3 * NB, LANES) for i in range(2)], axis=1
            )
            total = total + contract_last(lhs, row_pair(gath.at[0], r))
        g1part[p] = total * scale

        @pl.when(core == 1)
        def _():
            g1_copy(p).start()

    def rs_copy(owner, slot):
        return pltpu.make_async_remote_copy(
            src_ref=rs_send.at[owner], dst_ref=rs_recv.at[slot], send_sem=rs_sems.at[0, owner],
            recv_sem=rs_sems.at[1, slot],
            device_id={"space": owner * 2 + core}, device_id_type=MESH,
        )

    def to_owners(low, high):
        @pl.loop(low, high)
        def _(owner):
            @pl.when(owner == chip)
            def _():
                rs_recv[chip] = rs_send[chip]

            @pl.when(owner != chip)
            def _():
                rs_copy(owner, chip).start()

    def put_tiles(first, values):
        for i in range(values.shape[0] // 16):
            for half in range(2):
                tile = first + 2 * i + half
                rs_send[tile // TILES, tile % TILES] = values[
                    16 * i : 16 * i + 16, half * LANES : (half + 1) * LANES
                ].astype(BF16)

    @pl.when(core == 1)
    def _():
        @pl.loop(0, CH)
        def _(s):
            @pl.when((s != chan) | (chan < 4))
            def _():
                g2_copy(0, s).wait_recv()

        for k in range(3):
            loaded = [g2recv[s, k].astype(F32) for s in range(CH)]
            for t in range(4 * k, min(4 * k + 4, 9)):
                halves = []
                for half in range(2):
                    total = jnp.zeros((NB, LANES), F32)
                    for place in range(4):
                        moved = roll(loaded[4 * half + place], (place - t % 4) * NB)
                        total = jnp.where(lane // NB == place, moved, total)
                    halves.append(total)
                put_tiles(4 * t, jnp.concatenate(halves, axis=1))
        to_owners(0, OWNERS)

    @pl.when(core == 0)
    def _():
        for p in range(3):
            g1_copy(p).wait_recv()
            put_tiles(12 * p, g1part[p] + g1swap[p])
            to_owners(4 * p, 4 * p + 4)

    second_hops(hgath, hg_sems)
    turn_weights(0)

    def ag_copy(k, slot):
        return pltpu.make_async_remote_copy(
            src_ref=piece.at[slot], dst_ref=piece.at[slot], send_sem=ag_sems.at[0, k],
            recv_sem=ag_sems.at[1, slot],
            device_id={"space": lax.rem(chip + k, PEERS) * 2 + core}, device_id_type=MESH,
        )

    def sib_copy(slot):
        return remote(piece.at[slot], sib_in.at[slot], sib_sems, slot, space=sibling)

    @pl.when(chip < OWNERS)
    def _():
        @pl.loop(1, PEERS)
        def _(k):
            rs_copy(0, lax.rem(chip + k, PEERS)).wait_recv()

        total = rs_recv[0].astype(F32)
        for s in range(1, PEERS):
            total = total + rs_recv[s].astype(F32)
        piece[chip] = total.astype(BF16)

        @pl.loop(1, PEERS)
        def _(k):
            ag_copy(k, chip).start()

        sib_copy(chip).start()

    last_hops(hgath, hg_sems)
    products(lhs2[0], hgath, hgath[:, ROWS], prod)

    @pl.loop(0, NB // group_size)
    def _(group):
        main, _ = combine(prod, group, group_size)
        rows = group_rows(group, group_size)
        cot32[:, rows, :] = cot32[:, rows, :] + main.reshape(ROWS, group_size, LANES)

    out_ref[...] = cot32[...].astype(BF16)

    @pl.loop(1, PEERS)
    def _(k):
        source = lax.rem(chip + k, PEERS)

        @pl.when(source < OWNERS)
        def _():
            ag_copy(k, source).wait_recv()
            sib_copy(source).start()

    @pl.loop(0, OWNERS)
    def _(source):
        sib_copy(source).wait_recv()

    for tile in range(4 * 9):
        rows = slice(tile // 2 * 16, tile // 2 * 16 + 16)
        lanes = slice(tile % 2 * LANES, (tile % 2 + 1) * LANES)
        grads_ref[core, rows, lanes] = piece[tile // TILES, tile % TILES]
        grads_ref[1 - core, rows, lanes] = sib_in[tile // TILES, tile % TILES]

    to_left.wait_send()
    to_right.wait_send()
    w_out.wait_send()
    g2_swap.wait_send()
    for buf, sems in ((gath.at[0], main_sems.at[0]), (gath.at[1], main_sems.at[1]), (hgath, hg_sems)):
        for j in range(len(HOPS)):
            hop(buf, sems, j).wait_send()

    @pl.loop(1, CH)
    def _(k):
        halo_copy(k, chan).wait_send()
        w_copy(k, chan_at(k), chan).wait_send()

    for j in range(4):
        @pl.when((core == 0) | (core * 4 + j != chan))
        def _():
            g2_sent(j).wait_send()

    @pl.when(core == 1)
    def _():
        for p in range(3):
            g1_copy(p).wait_send()

    @pl.loop(0, OWNERS)
    def _(owner):
        sib_copy(owner).wait_send()

        @pl.when(owner != chip)
        def _():
            rs_copy(owner, chip).wait_send()

    @pl.when(chip < OWNERS)
    def _():
        @pl.loop(1, PEERS)
        def _(k):
            ag_copy(k, chip).wait_send()


def on_device(field, first_weight, second_weight, cotangent):
    vmem = pl.BlockSpec(memory_space=pltpu.VMEM)
    hbm = pl.BlockSpec(memory_space=pl.ANY)
    dma = pltpu.SemaphoreType.DMA
    out, grads = pl.pallas_call(
        kernel,
        out_shape=(
            jax.ShapeDtypeStruct((ROWS, NB, LANES), BF16),
            jax.ShapeDtypeStruct((2, 9 * NB, CH * NB), BF16),
        ),
        in_specs=[hbm] * 4,
        out_specs=(vmem, vmem),
        scratch_shapes=[
            pltpu.VMEM((NB, ROWS, LANES), BF16),
            pltpu.VMEM((NB, ROWS, LANES), BF16),
            pltpu.VMEM((9, NB, CH * NB), BF16),
            pltpu.VMEM((9, NB, CH * NB), BF16),
            pltpu.VMEM((NB * ROWS, LANES), F32),
            pltpu.VMEM((2, CH, ROWS, NB, LANES), BF16),
            pltpu.VMEM((CH, NB, LANES), BF16),
            pltpu.VMEM((NB, LANES), BF16),
            pltpu.VMEM((2, NB, LANES), BF16),
            pltpu.VMEM((ROWS, NB, LANES), F32),
            pltpu.VMEM((2, 9 * NB, CH * NB), BF16),
            pltpu.VMEM((CH, 3, NB, LANES), BF16),
            pltpu.VMEM((2, CH, 3, NB, LANES), BF16),
            pltpu.VMEM((ROWS + 1, 9 * NB, LANES), F32),
            pltpu.VMEM((2, 4, ROWS, NB, LANES), F32),
            pltpu.VMEM((3, ROWS + 2, NB, LANES), F32),
            pltpu.VMEM((2, 3, ROWS + 2, NB, LANES), BF16),
            pltpu.VMEM((NB, LANES), F32),
            pltpu.VMEM((CH, ROWS + 1, NB, LANES), BF16),
            pltpu.VMEM((CH, 3, NB, LANES), F32),
            pltpu.VMEM((4, 3, NB, LANES), F32),
            pltpu.VMEM((4, 3, NB, LANES), BF16),
            pltpu.VMEM((CH, 3, NB, LANES), BF16),
            pltpu.VMEM((3, 3 * NB, CH * NB), F32),
            pltpu.VMEM((3, 3 * NB, CH * NB), F32),
            pltpu.VMEM((OWNERS, TILES, 16, LANES), BF16),
            pltpu.VMEM((PEERS, TILES, 16, LANES), BF16),
            pltpu.VMEM((OWNERS, TILES, 16, LANES), BF16),
            pltpu.VMEM((OWNERS, TILES, 16, LANES), BF16),
            dma((4,)),
            dma((2, 2)),
            dma((2, 2, len(HOPS))),
            dma((2, CH)),
            dma((2, CH)),
            dma((2, 1)),
            dma((2, len(HOPS))),
            dma((2, 1)),
            dma((2, CH)),
            dma((2, 3)),
            dma((2, PEERS)),
            dma((2, PEERS)),
            dma((2, OWNERS)),
        ],
        compiler_params=pltpu.CompilerParams(
            collective_id=0, has_side_effects=True, vmem_limit_bytes=40 * 1024 * 1024
        ),
    )(field, first_weight.transpose(1, 0, 2), second_weight.transpose(1, 0, 2), cotangent)
    field_grad = out.transpose(1, 0, 2)
    grads = grads.astype(F32).reshape(2, 9, NB, CH * NB).transpose(0, 2, 1, 3)
    return (field_grad, grads[0], grads[1])


def solution(mesh):
    in_specs = (
        P("chan", None, "space"),
        P("chan", None, None),
        P("chan", None, None),
        P("chan", None, "space"),
    )
    out_specs = (P("chan", None, "space"), P("chan", None, None), P("chan", None, None))
    return jax.shard_map(
        on_device, mesh=mesh, in_specs=in_specs, out_specs=out_specs, check_vma=False
    )
```

time: 69.7 us -> 58.1 us (0.83)
  Pallas kernels: 65.4 us -> 52.2 us
  local copies, waits for them, and re-layouts: 3.4 us -> 5 us
    pallas_call x1, Pallas kernels: 65.4 us -> 52.2 us  [on_device(): pl.pallas_call(kernel, out_shape=(jax.ShapeDtypeStruct((ROWS, NB, LANES),...]
    unnamed x9, local copies, waits for them, and re-layouts: 2.55 us -> 4.15 us
where the time goes in v2:
time: 58.1 us; the launch traced here: 57.9 us
  Pallas kernels  52.2 us (90%)
  local copies, waits for them, and re-layouts  5 us (9%)
  between operations  0.66 us (1%)
    pallas_call x1, Pallas kernels, on_device(): pl.pallas_call(kernel, out_shape=(jax.ShapeDtypeStruct((ROWS, NB, LANES),...  52.2 us
    unnamed x9, local copies, waits for them, and re-layouts  4.15 us

profile of v2, /device:TPU:1, one launch (start us, length us, event | category | flops | bytes accessed | tf_op | source)
XLA Modules:
  0.0 57.9 jit_solution(3730240357758550327)
XLA Ops:
  0.6 0.0 copy-start
  0.6 0.9 %copy-done = bf16[32,9,256]{2,0,1:T(8,128)(2,1)S(1)} copy-done((bf16[32,9,256]{2,0,1:T(8,128)(2,1)S(1)}, bf16[32,9,256]{2,0,1:T(8,128)(2,1)}, u32[]{:S(2)}) %copy-start) | copy-done | bytes 147480
  1.5 0.0 copy-start.1
  1.5 0.9 %copy-done.1 = bf16[32,9,256]{2,0,1:T(8,128)(2,1)S(1)} copy-done((bf16[32,9,256]{2,0,1:T(8,128)(2,1)S(1)}, bf16[32,9,256]{2,0,1:T(8,128)(2,1)}, u32[]{:S(2)}) %copy-start.1) | copy-done | bytes 147480
  2.5 0.0 copy-start.2
  2.5 0.8 %copy-done.2 = bf16[32,8,128]{2,1,0:T(8,128)(2,1)S(1)} copy-done((bf16[32,8,128]{2,1,0:T(8,128)(2,1)S(1)}, bf16[32,8,128]{2,1,0:T(8,128)(2,1)}, u32[]{:S(2)}) %copy-start.2) | copy-done | bytes 65560
  3.3 0.0 copy-start.3
  3.3 0.8 %copy-done.3 = bf16[32,8,128]{2,1,0:T(8,128)(2,1)S(1)} copy-done((bf16[32,8,128]{2,1,0:T(8,128)(2,1)S(1)}, bf16[32,8,128]{2,1,0:T(8,128)(2,1)}, u32[]{:S(2)}) %copy-start.3) | copy-done | bytes 65560
  4.1 52.2 %shard_map.67 = (bf16[8,32,128]{2,1,0:T(8,128)(2,1)S(1)}, bf16[2,288,256]{2,1,0:T(8,128)(2,1)S(1)}) custom-call(bf16[32,8,128]{2,1,0:T(8,128)(2,1)S(1)} %copy-done.2, bf16[9,32,256]{2,1,0:T(8,128)(2,1)S(1)} %bitcast.12, bf16[9,32,256]{2,1,0:T(8,128)(2,1)S(1)} %bitcast.13, bf16[32,8,128]{2,1,0:T(8,128)(2,1)S(1)} %copy-done.3), custom_call_target="tpu_custom_call" | custom-call | tf_op jit(solution)/shard_map/pallas_call | solution.py:622
  56.4 0.7 %copy.7 = bf16[32,8,128]{2,1,0:T(8,128)(2,1)} copy(bf16[32,8,128]{2,0,1:T(8,128)(2,1)S(1)} %bitcast.14) | data formatting | bytes 131072
  57.1 0.9 %slice_bitcast_fusion = (f32[32,9,256]{2,0,1:T(8,128)}, f32[32,9,256]{2,0,1:T(8,128)}) fusion(f32[2,32,9,256]{3,1,2,0:T(8,128)S(1)} %convert_bitcast_fusion), kind=kLoop, calls=%fused_computation.1 | loop fusion | bytes 1179648 | tf_op jit(solution)/shard_map/squeeze | solution.py:680
  (1 shorter events, 0.0 us)
Async XLA Ops:
  0.6 0.9 %copy-start = (bf16[32,9,256]{2,0,1:T(8,128)(2,1)S(1)}, bf16[32,9,256]{2,0,1:T(8,128)(2,1)}, u32[]{:S(2)}) copy-start(bf16[32,9,256]{2,0,1:T(8,128)(2,1)} %param.5) | copy-start | bytes 442372
  1.5 0.9 %copy-start.1 = (bf16[32,9,256]{2,0,1:T(8,128)(2,1)S(1)}, bf16[32,9,256]{2,0,1:T(8,128)(2,1)}, u32[]{:S(2)}) copy-start(bf16[32,9,256]{2,0,1:T(8,128)(2,1)} %param.6) | copy-start | bytes 442372
  2.5 0.8 %copy-start.2 = (bf16[32,8,128]{2,1,0:T(8,128)(2,1)S(1)}, bf16[32,8,128]{2,1,0:T(8,128)(2,1)}, u32[]{:S(2)}) copy-start(bf16[32,8,128]{2,1,0:T(8,128)(2,1)} %field_hbm.1) | copy-start | bytes 196612
  3.3 0.8 %copy-start.3 = (bf16[32,8,128]{2,1,0:T(8,128)(2,1)S(1)}, bf16[32,8,128]{2,1,0:T(8,128)(2,1)}, u32[]{:S(2)}) copy-start(bf16[32,8,128]{2,1,0:T(8,128)(2,1)} %cot_hbm.1) | copy-start | bytes 196612

commit v3 on v2

--- a/solution.py
+++ b/solution.py
@@ -17,7 +17,7 @@
 LANES = 128
 PEERS = SP // 2
 OWNERS = 12
-TILES = 3
+PIECE = 48
 TAPS = [(p, q) for p in (-1, 0, 1) for q in (-1, 0, 1)]
 
 
@@ -211,12 +211,12 @@
 
 
 def kernel(
-    field_hbm, w1_hbm, w2_hbm, cot_hbm, out_ref, grads_ref,
+    field_hbm, w1_hbm, w2_hbm, cot_hbm, out_ref, g1_ref, g2_ref,
     field_in, cot_in, w1_in, w_in,
     rows32, gath, halo, edge, edge_in, cot32, lhs2, wsend, wrecv,
     prod, slopes, shifted32, shifted, packed32, hgath,
-    g2part, g2swap, g2send, g2recv, g1part, g1swap, rs_send, rs_recv, piece, sib_in,
-    in_sems, edge_sems, main_sems, halo_sems, w_sems, wsib_sems, hg_sems, g2swap_sems, g2_sems,
+    g2part, g2swap, g2send, g2recv, g1part, g1swap, rs_send, rs_recv, sums, sib_in,
+    in_sems, edge_sems, main_sems, halo_sems, w_sems, tile_sems, wsib_sems, hg_sems, g2swap_sems, g2_sems,
     g1_sems, rs_sems, ag_sems, sib_sems,
 ):
     chan = lax.axis_index("chan")
@@ -224,6 +224,7 @@
     core = lax.rem(space, 2)
     chip = lax.div(space, 2)
     line, level = lax.div(chan, 2), lax.rem(chan, 2)
+    column = lax.rem(chip, 4)
     left = lax.rem(space + SP - 1, SP)
     right = lax.rem(space + 1, SP)
     sibling = space + 1 - 2 * core
@@ -237,28 +238,29 @@
         at = 1 - level if other else level
         return lax.rem(line + step + 4, 4) * 2 + at
 
+    def fetch(src, dst, k):
+        return pltpu.make_async_copy(src, dst, in_sems.at[k])
+
+    fetch(field_hbm, field_in, 0).start()
+    fetch(cot_hbm, cot_in, 1).start()
+
     barrier = pltpu.get_barrier_semaphore()
 
     def greet(**target):
         pl.semaphore_signal(barrier, inc=1, device_id=target, device_id_type=MESH)
-
-    greet(space=left)
-    greet(space=right)
 
     @pl.loop(1, CH)
     def _(k):
         greet(chan=chan_at(k))
         greet(chan=chan_at(k), space=sibling)
 
+    greet(space=left)
+    greet(space=right)
+
     @pl.loop(1, PEERS)
     def _(k):
         greet(space=lax.rem(chip + k, PEERS) * 2 + core)
 
-    def fetch(src, dst, k):
-        return pltpu.make_async_copy(src, dst, in_sems.at[k])
-
-    fetch(field_hbm, field_in, 0).start()
-    fetch(cot_hbm, cot_in, 1).start()
     fetch(w1_hbm, w1_in, 2).start()
 
     @pl.when(core == 0)
@@ -302,50 +304,57 @@
         rows32[...] = source[...].astype(F32).reshape(NB * ROWS, LANES)
         return [rows32[pl.ds(r, NB, stride=ROWS), :] for r in range(ROWS)]
 
+    lane = lane_ids((NB, LANES))
     fetch(field_hbm, field_in, 0).wait()
     field_rows = split_rows(field_in)
     for r in range(ROWS):
         gath[0, chan, r] = field_rows[r].astype(BF16)
-
-    pl.semaphore_wait(barrier, 2 * (CH - 1) + PEERS - 1 + 2)
-    first_hops(gath.at[0], main_sems.at[0])
-
+    edge_field = pack(field_rows)
     fetch(cot_hbm, cot_in, 1).wait()
-    edge_field = pack(field_rows)
     cot_rows = split_rows(cot_in)
     for r in range(ROWS):
         gath[1, chan, r] = cot_rows[r].astype(BF16)
         cot32[r] = cot_rows[r]
-    lane = lane_ids((NB, LANES))
     near = (lane % 16 < 4) | (lane % 16 >= 12)
     edge[...] = jnp.where(near, edge_field, roll(pack(cot_rows), 8)).astype(BF16)
+
+    fetch(w1_hbm, w1_in, 2).wait()
+    fetch(w1_hbm, w_in, 3).wait()
+
+    def w_copy(k, dest, slot):
+        return remote(wsend.at[dest], wrecv.at[core, column, slot], w_sems, k, chan=chan_at(k))
+
+    @pl.when(column < 3)
+    def _():
+        loaded = [
+            jnp.where(
+                4 * column + u < 9, w_in[jnp.maximum(8 - 4 * column - u, 0)].astype(F32), 0.0
+            )
+            for u in range(4)
+        ]
+        for dest in range(CH):
+            half, place = dest // 4, dest % 4
+            total = jnp.zeros((NB, LANES), F32)
+            for u, values in enumerate(loaded):
+                source = values[:, half * LANES : (half + 1) * LANES]
+                total = jnp.where(lane // NB == u, roll(source, (u - place) * NB), total)
+            wsend[dest] = total.astype(BF16)
+        wrecv[core, column, chan] = wsend[chan]
+
+    pl.semaphore_wait(barrier, 2 * (CH - 1) + PEERS - 1 + 2)
+
     to_left = remote(edge, edge_in.at[0], edge_sems, 0, space=left)
     to_right = remote(edge, edge_in.at[1], edge_sems, 1, space=right)
     to_left.start()
     to_right.start()
-    first_hops(gath.at[1], main_sems.at[1])
-
-    fetch(w1_hbm, w1_in, 2).wait()
-    fetch(w1_hbm, w_in, 3).wait()
-    for k in range(3):
-        taps = range(4 * k, min(4 * k + 4, 9))
-        loaded = [w_in[8 - t].astype(F32) for t in taps]
-        for dest in range(CH):
-            half, place = dest // 4, dest % 4
-            total = jnp.zeros((NB, LANES), F32)
-            for t, values in zip(taps, loaded):
-                source = values[:, half * LANES : (half + 1) * LANES]
-                total = jnp.where(lane // NB == t % 4, roll(source, (t % 4 - place) * NB), total)
-            wsend[dest, k] = total.astype(BF16)
-
-    def w_copy(k, dest, slot):
-        return remote(wsend.at[dest], wrecv.at[core, slot], w_sems, k, chan=chan_at(k))
-
-    @pl.loop(1, CH)
-    def _(k):
-        w_copy(k, chan_at(k), chan).start()
-
-    wrecv[core, chan] = wsend[chan]
+
+    @pl.when(column < 3)
+    def _():
+        @pl.loop(1, CH)
+        def _(k):
+            w_copy(k, chan_at(k), chan).start()
+
+    first_hops(gath.at[0], main_sems.at[0])
 
     to_left.wait_recv()
     to_right.wait_recv()
@@ -360,8 +369,36 @@
     def _(k):
         halo_copy(k, chan).start()
 
+    first_hops(gath.at[1], main_sems.at[1])
+
+    def tile_copy(k, tile):
+        target = (chip - column + lax.rem(column + k, 4)) * 2 + core
+        return pltpu.make_async_remote_copy(
+            src_ref=wrecv.at[core, tile], dst_ref=wrecv.at[core, tile], send_sem=tile_sems.at[0, k],
+            recv_sem=tile_sems.at[1, tile], device_id={"space": target}, device_id_type=MESH,
+        )
+
+    @pl.when(column < 3)
+    def _():
+        @pl.loop(1, CH)
+        def _(k):
+            w_copy(k, chan_at(k), chan_at(CH - k)).wait_recv()
+
+        @pl.loop(1, 4)
+        def _(k):
+            tile_copy(k, column).start()
+
     second_hops(gath.at[0], main_sems.at[0])
     second_hops(gath.at[1], main_sems.at[1])
+
+    @pl.loop(0, 3)
+    def _(tile):
+        @pl.when(tile != column)
+        def _():
+            tile_copy(1, tile).wait_recv()
+
+    w_out = remote(wrecv.at[core], wrecv.at[core], wsib_sems, 0, space=sibling)
+    w_out.start()
 
     last_hops(gath.at[0], main_sems.at[0])
 
@@ -379,13 +416,6 @@
         resample_forward(prod, group, group_size, slopes, shifted32)
 
     shifted[0] = shifted32[...].astype(BF16)
-
-    @pl.loop(1, CH)
-    def _(k):
-        w_copy(k, chan_at(k), chan_at(CH - k)).wait_recv()
-
-    w_out = remote(wrecv.at[core], wrecv.at[core], wsib_sems, 0, space=sibling)
-    w_out.start()
 
     last_hops(gath.at[1], main_sems.at[1])
     total = jnp.zeros((CH * NB, 3 * LANES), F32)
@@ -404,7 +434,7 @@
 
     def turn_weights(which):
         for k in range(3):
-            turned = wrecv[which, :, k].reshape(CH * NB, LANES).T
+            turned = wrecv[which, k].reshape(CH * NB, LANES).T
             if k < 2:
                 lhs2[which, k * LANES : (k + 1) * LANES, :] = turned
             else:
@@ -463,9 +493,13 @@
         def _():
             g1_copy(p).start()
 
+    def piece_of(ref, owner):
+        rows = pl.ds(pl.multiple_of(lax.div(owner, 2) * PIECE, 16), PIECE)
+        return ref.at[lax.rem(owner, 2), rows]
+
     def rs_copy(owner, slot):
         return pltpu.make_async_remote_copy(
-            src_ref=rs_send.at[owner], dst_ref=rs_recv.at[slot], send_sem=rs_sems.at[0, owner],
+            src_ref=piece_of(rs_send, owner), dst_ref=rs_recv.at[slot], send_sem=rs_sems.at[0, owner],
             recv_sem=rs_sems.at[1, slot],
             device_id={"space": owner * 2 + core}, device_id_type=MESH,
         )
@@ -475,19 +509,17 @@
         def _(owner):
             @pl.when(owner == chip)
             def _():
-                rs_recv[chip] = rs_send[chip]
+                rs_recv[chip] = piece_of(rs_send, chip)[...]
 
             @pl.when(owner != chip)
             def _():
                 rs_copy(owner, chip).start()
 
-    def put_tiles(first, values):
-        for i in range(values.shape[0] // 16):
-            for half in range(2):
-                tile = first + 2 * i + half
-                rs_send[tile // TILES, tile % TILES] = values[
-                    16 * i : 16 * i + 16, half * LANES : (half + 1) * LANES
-                ].astype(BF16)
+    def put_rows(first, values):
+        for half in range(2):
+            rs_send[half, first : first + values.shape[0]] = values[
+                :, half * LANES : (half + 1) * LANES
+            ].astype(BF16)
 
     @pl.when(core == 1)
     def _():
@@ -500,21 +532,19 @@
         for k in range(3):
             loaded = [g2recv[s, k].astype(F32) for s in range(CH)]
             for t in range(4 * k, min(4 * k + 4, 9)):
-                halves = []
                 for half in range(2):
                     total = jnp.zeros((NB, LANES), F32)
                     for place in range(4):
                         moved = roll(loaded[4 * half + place], (place - t % 4) * NB)
                         total = jnp.where(lane // NB == place, moved, total)
-                    halves.append(total)
-                put_tiles(4 * t, jnp.concatenate(halves, axis=1))
+                    rs_send[half, t * NB : (t + 1) * NB] = total.astype(BF16)
         to_owners(0, OWNERS)
 
     @pl.when(core == 0)
     def _():
         for p in range(3):
             g1_copy(p).wait_recv()
-            put_tiles(12 * p, g1part[p] + g1swap[p])
+            put_rows(96 * p, g1part[p] + g1swap[p])
             to_owners(4 * p, 4 * p + 4)
 
     second_hops(hgath, hg_sems)
@@ -522,13 +552,13 @@
 
     def ag_copy(k, slot):
         return pltpu.make_async_remote_copy(
-            src_ref=piece.at[slot], dst_ref=piece.at[slot], send_sem=ag_sems.at[0, k],
+            src_ref=piece_of(sums, slot), dst_ref=piece_of(sums, slot), send_sem=ag_sems.at[0, k],
             recv_sem=ag_sems.at[1, slot],
             device_id={"space": lax.rem(chip + k, PEERS) * 2 + core}, device_id_type=MESH,
         )
 
     def sib_copy(slot):
-        return remote(piece.at[slot], sib_in.at[slot], sib_sems, slot, space=sibling)
+        return remote(piece_of(sums, slot), piece_of(sib_in, slot), sib_sems, slot, space=sibling)
 
     @pl.when(chip < OWNERS)
     def _():
@@ -539,7 +569,7 @@
         total = rs_recv[0].astype(F32)
         for s in range(1, PEERS):
             total = total + rs_recv[s].astype(F32)
-        piece[chip] = total.astype(BF16)
+        piece_of(sums, chip)[...] = total.astype(BF16)
 
         @pl.loop(1, PEERS)
         def _(k):
@@ -556,7 +586,9 @@
         rows = group_rows(group, group_size)
         cot32[:, rows, :] = cot32[:, rows, :] + main.reshape(ROWS, group_size, LANES)
 
-    out_ref[...] = cot32[...].astype(BF16)
+    for r in range(ROWS):
+        rows32[pl.ds(r, NB, stride=ROWS), :] = cot32[r]
+    out_ref[...] = rows32[...].reshape(NB, ROWS, LANES).astype(BF16)
 
     @pl.loop(1, PEERS)
     def _(k):
@@ -567,15 +599,20 @@
             ag_copy(k, source).wait_recv()
             sib_copy(source).start()
 
+    def store(source, which):
+        for grad, ref in enumerate((g1_ref, g2_ref)):
+            @pl.when(which == grad)
+            def _():
+                for half in range(2):
+                    ref[:, half * LANES : (half + 1) * LANES] = source[half]
+
+    store(sums, core)
+
     @pl.loop(0, OWNERS)
     def _(source):
         sib_copy(source).wait_recv()
 
-    for tile in range(4 * 9):
-        rows = slice(tile // 2 * 16, tile // 2 * 16 + 16)
-        lanes = slice(tile % 2 * LANES, (tile % 2 + 1) * LANES)
-        grads_ref[core, rows, lanes] = piece[tile // TILES, tile % TILES]
-        grads_ref[1 - core, rows, lanes] = sib_in[tile // TILES, tile % TILES]
+    store(sib_in, 1 - core)
 
     to_left.wait_send()
     to_right.wait_send()
@@ -588,7 +625,16 @@
     @pl.loop(1, CH)
     def _(k):
         halo_copy(k, chan).wait_send()
-        w_copy(k, chan_at(k), chan).wait_send()
+
+    @pl.when(column < 3)
+    def _():
+        @pl.loop(1, CH)
+        def _(k):
+            w_copy(k, chan_at(k), chan).wait_send()
+
+        @pl.loop(1, 4)
+        def _(k):
+            tile_copy(k, column).wait_send()
 
     for j in range(4):
         @pl.when((core == 0) | (core * 4 + j != chan))
@@ -617,16 +663,17 @@
 
 def on_device(field, first_weight, second_weight, cotangent):
     vmem = pl.BlockSpec(memory_space=pltpu.VMEM)
-    hbm = pl.BlockSpec(memory_space=pl.ANY)
+    hbm = pl.BlockSpec(memory_space=pltpu.HBM)
     dma = pltpu.SemaphoreType.DMA
-    out, grads = pl.pallas_call(
+    out, first_grad, second_grad = pl.pallas_call(
         kernel,
         out_shape=(
-            jax.ShapeDtypeStruct((ROWS, NB, LANES), BF16),
-            jax.ShapeDtypeStruct((2, 9 * NB, CH * NB), BF16),
+            jax.ShapeDtypeStruct((NB, ROWS, LANES), BF16),
+            jax.ShapeDtypeStruct((9 * NB, CH * NB), BF16),
+            jax.ShapeDtypeStruct((9 * NB, CH * NB), BF16),
         ),
         in_specs=[hbm] * 4,
-        out_specs=(vmem, vmem),
+        out_specs=(vmem, vmem, vmem),
         scratch_shapes=[
             pltpu.VMEM((NB, ROWS, LANES), BF16),
             pltpu.VMEM((NB, ROWS, LANES), BF16),
@@ -639,8 +686,8 @@
             pltpu.VMEM((2, NB, LANES), BF16),
             pltpu.VMEM((ROWS, NB, LANES), F32),
             pltpu.VMEM((2, 9 * NB, CH * NB), BF16),
-            pltpu.VMEM((CH, 3, NB, LANES), BF16),
-            pltpu.VMEM((2, CH, 3, NB, LANES), BF16),
+            pltpu.VMEM((CH, NB, LANES), BF16),
+            pltpu.VMEM((2, 3, CH, NB, LANES), BF16),
             pltpu.VMEM((ROWS + 1, 9 * NB, LANES), F32),
             pltpu.VMEM((2, 4, ROWS, NB, LANES), F32),
             pltpu.VMEM((3, ROWS + 2, NB, LANES), F32),
@@ -653,15 +700,16 @@
             pltpu.VMEM((CH, 3, NB, LANES), BF16),
             pltpu.VMEM((3, 3 * NB, CH * NB), F32),
             pltpu.VMEM((3, 3 * NB, CH * NB), F32),
-            pltpu.VMEM((OWNERS, TILES, 16, LANES), BF16),
-            pltpu.VMEM((PEERS, TILES, 16, LANES), BF16),
-            pltpu.VMEM((OWNERS, TILES, 16, LANES), BF16),
-            pltpu.VMEM((OWNERS, TILES, 16, LANES), BF16),
+            pltpu.VMEM((2, 9 * NB, LANES), BF16),
+            pltpu.VMEM((PEERS, PIECE, LANES), BF16),
+            pltpu.VMEM((2, 9 * NB, LANES), BF16),
+            pltpu.VMEM((2, 9 * NB, LANES), BF16),
             dma((4,)),
             dma((2, 2)),
             dma((2, 2, len(HOPS))),
             dma((2, CH)),
             dma((2, CH)),
+            dma((2, 4)),
             dma((2, 1)),
             dma((2, len(HOPS))),
             dma((2, 1)),
@@ -674,10 +722,19 @@
         compiler_params=pltpu.CompilerParams(
             collective_id=0, has_side_effects=True, vmem_limit_bytes=40 * 1024 * 1024
         ),
-    )(field, first_weight.transpose(1, 0, 2), second_weight.transpose(1, 0, 2), cotangent)
-    field_grad = out.transpose(1, 0, 2)
-    grads = grads.astype(F32).reshape(2, 9, NB, CH * NB).transpose(0, 2, 1, 3)
-    return (field_grad, grads[0], grads[1])
+    )(
+        *(
+            pltpu.with_memory_space_constraint(x, pltpu.HBM)
+            for x in (
+                field, first_weight.transpose(1, 0, 2), second_weight.transpose(1, 0, 2), cotangent
+            )
+        )
+    )
+
+    def taps_inside(grad):
+        return grad.astype(F32).reshape(9, NB, CH * NB).transpose(1, 0, 2)
+
+    return (out, taps_inside(first_grad), taps_inside(second_grad))
 
 
 def solution(mesh):

time: 58.1 us -> 54.3 us (0.935)
  local copies, waits for them, and re-layouts: 5 us -> 0.63 us
  other arithmetic: 0.05 us -> 0.87 us
    unnamed x9 -> x1, local copies, waits for them, and re-layouts: 4.15 us -> 0.63 us
    squeeze x1 -> x0, local copies, waits for them, and re-layouts: 0.85 us -> none  [on_device(): return (field_grad, grads[0], grads[1])]
    transpose x1, other arithmetic: 0.05 us -> 0.87 us  [taps_inside(): return grad.astype(F32).reshape(9, NB, CH * NB).transpose(1, 0, 2)]
where the time goes in v3:
time: 54.3 us; the launch traced here: 54.2 us
  Pallas kernels  52 us (96%)
  other arithmetic  0.87 us (2%)
  between operations  0.64 us (1%)
  local copies, waits for them, and re-layouts  0.63 us (1%)
    pallas_call x1, Pallas kernels, on_device(): pl.pallas_call(kernel, out_shape=(jax.ShapeDtypeStruct((NB, ROWS, LANES),...  52 us

profile of v3, /device:TPU:1, one launch (start us, length us, event | category | flops | bytes accessed | tf_op | source)
XLA Modules:
  0.0 54.2 jit_solution(8437081848393693753)
XLA Ops:
  0.6 52.0 %shard_map.67 = (bf16[32,8,128]{2,1,0:T(8,128)(2,1)S(1)}, bf16[288,256]{1,0:T(8,128)(2,1)S(1)}, bf16[288,256]{1,0:T(8,128)(2,1)S(1)}) custom-call(bf16[32,8,128]{2,1,0:T(8,128)(2,1)} %field_hbm.1, bf16[9,32,256]{2,1,0:T(8,128)(2,1)} %bitcast.12, bf16[9,32,256]{2,1,0:T(8,128)(2,1)} %bitcast.13, bf16[32,8,128]{2,1,0:T(8,128)(2,1)} %cot_hbm.1), custom_call_target="tpu_custom_call" | custom-call | tf_op jit(solution)/shard_map/pallas_call | solution.py:668
  52.7 0.9 %convert_bitcast_fusion = (f32[32,9,256]{2,0,1:T(8,128)}, f32[32,9,256]{2,0,1:T(8,128)}) fusion(bf16[9,32,256]{2,1,0:T(8,128)(2,1)S(1)} %bitcast.11, bf16[9,32,256]{2,1,0:T(8,128)(2,1)S(1)} %bitcast.10), kind=kLoop, calls=%fused_computation | loop fusion | flops 147456 | bytes 884736 | tf_op jit(solution)/shard_map/transpose | solution.py:735
  53.5 0.6 %copy.8 = bf16[32,8,128]{2,1,0:T(8,128)(2,1)} copy(bf16[32,8,128]{2,1,0:T(8,128)(2,1)S(1)} %get-tuple-element.14) | data formatting | bytes 131072

commit v4 on v3

--- a/solution.py
+++ b/solution.py
@@ -199,6 +199,11 @@
     return lax.dot_general(a, b, (((1,), (1,)), ((), ())), preferred_element_type=F32)
 
 
+NEAREST = sorted(
+    ((dz, dx) for dz in range(4) for dx in range(4) if dz or dx),
+    key=lambda d: (2 * min(d[0], 4 - d[0]) + min(d[1], 4 - d[1]), d),
+)
+
 HOPS = (
     ((0, 0), (1, 0), (-1, 0)),
     ((0, 0), (-1, 0), (1, 0)),
@@ -225,6 +230,7 @@
     chip = lax.div(space, 2)
     line, level = lax.div(chan, 2), lax.rem(chan, 2)
     column = lax.rem(chip, 4)
+    plane = lax.div(chip, 4)
     left = lax.rem(space + SP - 1, SP)
     right = lax.rem(space + 1, SP)
     sibling = space + 1 - 2 * core
@@ -233,6 +239,10 @@
     def chan_at(k):
         return lax.rem(chan + k, CH)
 
+    def chip_at(k):
+        dz, dx = NEAREST[k]
+        return lax.rem(plane + dz, 4) * 4 + lax.rem(column + dx, 4)
+
     def block_at(place):
         step, other = place
         at = 1 - level if other else level
@@ -285,20 +295,22 @@
         got = block_at(HOPS[j][2])
         return remote(buf.at[got], buf.at[got], sems, j, chan=block_at(HOPS[j][1]))
 
-    def first_hops(buf, sems):
-        for j in range(4):
+    def send(buf, sems, *hops):
+        for j in hops:
             hop(buf, sems, j).start()
 
+    def arrive(buf, sems, *hops):
+        for j in hops:
+            hop_in(buf, sems, j).wait_recv()
+
     def second_hops(buf, sems):
-        hop_in(buf, sems, 2).wait_recv()
-        hop(buf, sems, 4).start()
-        hop(buf, sems, 5).start()
-        hop_in(buf, sems, 3).wait_recv()
-        hop(buf, sems, 6).start()
+        arrive(buf, sems, 2)
+        send(buf, sems, 4, 5)
+        arrive(buf, sems, 3)
+        send(buf, sems, 6)
 
     def last_hops(buf, sems):
-        for j in (0, 1, 4, 5, 6):
-            hop_in(buf, sems, j).wait_recv()
+        arrive(buf, sems, 0, 1, 4, 5, 6)
 
     def split_rows(source):
         rows32[...] = source[...].astype(F32).reshape(NB * ROWS, LANES)
@@ -354,7 +366,10 @@
         def _(k):
             w_copy(k, chan_at(k), chan).start()
 
-    first_hops(gath.at[0], main_sems.at[0])
+    field_all, cot_all = (gath.at[0], main_sems.at[0]), (gath.at[1], main_sems.at[1])
+    send(*field_all, 3, 2)
+    send(*cot_all, 3, 2)
+    send(*field_all, 0, 1)
 
     to_left.wait_recv()
     to_right.wait_recv()
@@ -369,8 +384,6 @@
     def _(k):
         halo_copy(k, chan).start()
 
-    first_hops(gath.at[1], main_sems.at[1])
-
     def tile_copy(k, tile):
         target = (chip - column + lax.rem(column + k, 4)) * 2 + core
         return pltpu.make_async_remote_copy(
@@ -378,6 +391,9 @@
             recv_sem=tile_sems.at[1, tile], device_id={"space": target}, device_id_type=MESH,
         )
 
+    second_hops(*field_all)
+    send(*cot_all, 0, 1)
+
     @pl.when(column < 3)
     def _():
         @pl.loop(1, CH)
@@ -388,8 +404,7 @@
         def _(k):
             tile_copy(k, column).start()
 
-    second_hops(gath.at[0], main_sems.at[0])
-    second_hops(gath.at[1], main_sems.at[1])
+    second_hops(*cot_all)
 
     @pl.loop(0, 3)
     def _(tile):
@@ -400,7 +415,7 @@
     w_out = remote(wrecv.at[core], wrecv.at[core], wsib_sems, 0, space=sibling)
     w_out.start()
 
-    last_hops(gath.at[0], main_sems.at[0])
+    last_hops(*field_all)
 
     @pl.loop(1, CH)
     def _(k):
@@ -417,7 +432,7 @@
 
     shifted[0] = shifted32[...].astype(BF16)
 
-    last_hops(gath.at[1], main_sems.at[1])
+    last_hops(*cot_all)
     total = jnp.zeros((CH * NB, 3 * LANES), F32)
     for r in range(0, ROWS, 2):
         rhs = tap_row_pair(shifted.at[0], r, 1)
@@ -475,7 +490,7 @@
     shifted[1] = shifted32[...].astype(BF16)
     hgath[chan, 0:ROWS] = shifted[1, 1, 1 : ROWS + 1]
     hgath[chan, ROWS] = packed32[...].astype(BF16)
-    first_hops(hgath, hg_sems)
+    send(hgath, hg_sems, 3, 2, 0, 1)
 
     def g1_copy(p):
         return remote(g1part.at[p], g1swap.at[p], g1_sems, p, space=sibling)
@@ -554,7 +569,7 @@
         return pltpu.make_async_remote_copy(
             src_ref=piece_of(sums, slot), dst_ref=piece_of(sums, slot), send_sem=ag_sems.at[0, k],
             recv_sem=ag_sems.at[1, slot],
-            device_id={"space": lax.rem(chip + k, PEERS) * 2 + core}, device_id_type=MESH,
+            device_id={"space": chip_at(k) * 2 + core}, device_id_type=MESH,
         )
 
     def sib_copy(slot):
@@ -571,10 +586,8 @@
             total = total + rs_recv[s].astype(F32)
         piece_of(sums, chip)[...] = total.astype(BF16)
 
-        @pl.loop(1, PEERS)
-        def _(k):
+        for k in reversed(range(PEERS - 1)):
             ag_copy(k, chip).start()
-
         sib_copy(chip).start()
 
     last_hops(hgath, hg_sems)
@@ -590,9 +603,8 @@
         rows32[pl.ds(r, NB, stride=ROWS), :] = cot32[r]
     out_ref[...] = rows32[...].reshape(NB, ROWS, LANES).astype(BF16)
 
-    @pl.loop(1, PEERS)
-    def _(k):
-        source = lax.rem(chip + k, PEERS)
+    for k in range(PEERS - 1):
+        source = chip_at(k)
 
         @pl.when(source < OWNERS)
         def _():
@@ -656,8 +668,7 @@
 
     @pl.when(chip < OWNERS)
     def _():
-        @pl.loop(1, PEERS)
-        def _(k):
+        for k in range(PEERS - 1):
             ag_copy(k, chip).wait_send()
 
 

time: 54.3 us -> 50.7 us (0.934)
  Pallas kernels: 52 us -> 48.4 us
    pallas_call x1, Pallas kernels: 52 us -> 48.4 us  [on_device(): pl.pallas_call(kernel, out_shape=(jax.ShapeDtypeStruct((NB, ROWS, LANES),...]
where the time goes in v4:
time: 50.7 us; the launch traced here: 50.6 us
  Pallas kernels  48.4 us (95%)
  other arithmetic  0.87 us (2%)
  between operations  0.64 us (1%)
  local copies, waits for them, and re-layouts  0.63 us (1%)
    pallas_call x1, Pallas kernels, on_device(): pl.pallas_call(kernel, out_shape=(jax.ShapeDtypeStruct((NB, ROWS, LANES),...  48.4 us

profile of v4, /device:TPU:1, one launch (start us, length us, event | category | flops | bytes accessed | tf_op | source)
XLA Modules:
  0.0 50.6 jit_solution(11633548821438928803)
XLA Ops:
  0.6 48.4 %shard_map.67 = (bf16[32,8,128]{2,1,0:T(8,128)(2,1)S(1)}, bf16[288,256]{1,0:T(8,128)(2,1)S(1)}, bf16[288,256]{1,0:T(8,128)(2,1)S(1)}) custom-call(bf16[32,8,128]{2,1,0:T(8,128)(2,1)} %field_hbm.1, bf16[9,32,256]{2,1,0:T(8,128)(2,1)} %bitcast.12, bf16[9,32,256]{2,1,0:T(8,128)(2,1)} %bitcast.13, bf16[32,8,128]{2,1,0:T(8,128)(2,1)} %cot_hbm.1), custom_call_target="tpu_custom_call" | custom-call | tf_op jit(solution)/shard_map/pallas_call | solution.py:679
  49.1 0.9 %convert_bitcast_fusion = (f32[32,9,256]{2,0,1:T(8,128)}, f32[32,9,256]{2,0,1:T(8,128)}) fusion(bf16[9,32,256]{2,1,0:T(8,128)(2,1)S(1)} %bitcast.11, bf16[9,32,256]{2,1,0:T(8,128)(2,1)S(1)} %bitcast.10), kind=kLoop, calls=%fused_computation | loop fusion | flops 147456 | bytes 884736 | tf_op jit(solution)/shard_map/transpose | solution.py:746
  49.9 0.6 %copy.8 = bf16[32,8,128]{2,1,0:T(8,128)(2,1)} copy(bf16[32,8,128]{2,1,0:T(8,128)(2,1)S(1)} %get-tuple-element.14) | data formatting | bytes 131072

commit v5 on v4

--- a/solution.py
+++ b/solution.py
@@ -212,6 +212,7 @@
     ((0, 1), (1, 0), (-1, 1)),
     ((0, 1), (-1, 0), (1, 1)),
     ((2, 0), (0, 1), (2, 1)),
+    ((0, 1), (2, 0), (2, 1)),
 )
 
 
@@ -220,8 +221,8 @@
     field_in, cot_in, w1_in, w_in,
     rows32, gath, halo, edge, edge_in, cot32, lhs2, wsend, wrecv,
     prod, slopes, shifted32, shifted, packed32, hgath,
-    g2part, g2swap, g2send, g2recv, g1part, g1swap, rs_send, rs_recv, sums, sib_in,
-    in_sems, edge_sems, main_sems, halo_sems, w_sems, tile_sems, wsib_sems, hg_sems, g2swap_sems, g2_sems,
+    g2send, g2recv, g1part, g1swap, rs_send, rs_recv, sums, sib_in,
+    in_sems, edge_sems, main_sems, halo_sems, w_sems, tile_sems, wsib_sems, hg_sems, g2_sems,
     g1_sems, rs_sems, ag_sems, sib_sems,
 ):
     chan = lax.axis_index("chan")
@@ -421,7 +422,7 @@
     def _(k):
         halo_copy(k, chan_at(CH - k)).wait_recv()
 
-    group_size = 8
+    group_size = 16
     shifted32[:, 0] = jnp.zeros((3, NB, LANES), F32)
     shifted32[:, ROWS + 1] = jnp.zeros((3, NB, LANES), F32)
     products(w1_in[...].reshape(9 * NB, CH * NB), gath.at[0], halo[...], prod)
@@ -438,12 +439,28 @@
         rhs = tap_row_pair(shifted.at[0], r, 1)
         rhs = jnp.concatenate([rhs, jnp.zeros((3 * NB, 2 * LANES), BF16)], axis=0)
         total = total + contract_last(row_pair(gath.at[1], r), rhs)
-    total = total * scale
+    total = (total * scale).astype(BF16)
     for k in range(3):
-        g2part[:, k] = total[:, k * LANES : (k + 1) * LANES].reshape(CH, NB, LANES)
-
-    g2_swap = remote(g2part.at[pl.ds(4 - 4 * core, 4)], g2swap, g2swap_sems, 0, space=sibling)
-    g2_swap.start()
+        g2send[:, k] = total[:, k * LANES : (k + 1) * LANES].reshape(CH, NB, LANES)
+
+    def g2_copy(dest, source_core, source):
+        return pltpu.make_async_remote_copy(
+            src_ref=g2send.at[dest], dst_ref=g2recv.at[source_core, source],
+            send_sem=g2_sems.at[0, 0, dest], recv_sem=g2_sems.at[1, source_core, source],
+            device_id={"chan": dest, "space": 2 * chip + 1}, device_id_type=MESH,
+        )
+
+    @pl.loop(1, CH)
+    def _(k):
+        g2_copy(chan_at(k), core, chan).start()
+
+    @pl.when(core == 0)
+    def _():
+        g2_copy(chan, core, chan).start()
+
+    @pl.when(core == 1)
+    def _():
+        g2recv[1, chan] = g2send[chan]
 
     remote(wrecv.at[1 - core], wrecv.at[1 - core], wsib_sems, 0, space=sibling).wait_recv()
 
@@ -458,31 +475,6 @@
     turn_weights(1)
     products(lhs2[1], gath.at[1], halo[...], prod)
 
-    def g2_copy(j, slot):
-        return remote(
-            g2send.at[j], g2recv.at[slot], g2_sems, slot, chan=core * 4 + j, space=2 * chip + 1
-        )
-
-    def g2_sent(j):
-        return pltpu.make_async_remote_copy(
-            src_ref=g2send.at[j], dst_ref=g2recv.at[chan], send_sem=g2_sems.at[0, j],
-            recv_sem=g2_sems.at[1, chan],
-            device_id={"chan": core * 4 + j, "space": 2 * chip + 1}, device_id_type=MESH,
-        )
-
-    g2_swap.wait_recv()
-    for j in range(4):
-        g2send[j] = (g2part[core * 4 + j] + g2swap[j]).astype(BF16)
-        mine = (core == 1) & (core * 4 + j == chan)
-
-        @pl.when(mine)
-        def _():
-            g2recv[chan] = g2send[j]
-
-        @pl.when(jnp.logical_not(mine))
-        def _():
-            g2_sent(j).start()
-
     @pl.loop(0, NB // group_size)
     def _(group):
         resample_backward(prod, group, group_size, slopes, shifted32, packed32)
@@ -490,7 +482,7 @@
     shifted[1] = shifted32[...].astype(BF16)
     hgath[chan, 0:ROWS] = shifted[1, 1, 1 : ROWS + 1]
     hgath[chan, ROWS] = packed32[...].astype(BF16)
-    send(hgath, hg_sems, 3, 2, 0, 1)
+    send(hgath, hg_sems, *(2, 3, 0, 1))
 
     def g1_copy(p):
         return remote(g1part.at[p], g1swap.at[p], g1_sems, p, space=sibling)
@@ -512,11 +504,19 @@
         rows = pl.ds(pl.multiple_of(lax.div(owner, 2) * PIECE, 16), PIECE)
         return ref.at[lax.rem(owner, 2), rows]
 
-    def rs_copy(owner, slot):
+    def rs_copy(owner):
+        slot = lax.rem(chip - owner + PEERS, PEERS) - 1
         return pltpu.make_async_remote_copy(
-            src_ref=piece_of(rs_send, owner), dst_ref=rs_recv.at[slot], send_sem=rs_sems.at[0, owner],
-            recv_sem=rs_sems.at[1, slot],
+            src_ref=piece_of(rs_send, owner), dst_ref=rs_recv.at[slot], send_sem=rs_sems.at[0],
+            recv_sem=rs_sems.at[1],
             device_id={"space": owner * 2 + core}, device_id_type=MESH,
+        )
+
+    def all_pieces(count):
+        return pltpu.make_async_remote_copy(
+            src_ref=rs_recv.at[pl.ds(0, count)], dst_ref=rs_recv.at[pl.ds(0, count)],
+            send_sem=rs_sems.at[0], recv_sem=rs_sems.at[1],
+            device_id={"space": sibling}, device_id_type=MESH,
         )
 
     def to_owners(low, high):
@@ -524,11 +524,11 @@
         def _(owner):
             @pl.when(owner == chip)
             def _():
-                rs_recv[chip] = piece_of(rs_send, chip)[...]
+                rs_recv[PEERS - 1] = piece_of(rs_send, chip)[...]
 
             @pl.when(owner != chip)
             def _():
-                rs_copy(owner, chip).start()
+                rs_copy(owner).start()
 
     def put_rows(first, values):
         for half in range(2):
@@ -538,14 +538,17 @@
 
     @pl.when(core == 1)
     def _():
-        @pl.loop(0, CH)
-        def _(s):
-            @pl.when((s != chan) | (chan < 4))
-            def _():
-                g2_copy(0, s).wait_recv()
+        g2_copy(chan, 0, chan).wait_recv()
+
+        @pl.loop(1, CH)
+        def _(k):
+            for source_core in range(2):
+                g2_copy(chan, source_core, chan_at(k)).wait_recv()
 
         for k in range(3):
-            loaded = [g2recv[s, k].astype(F32) for s in range(CH)]
+            loaded = [
+                g2recv[0, s, k].astype(F32) + g2recv[1, s, k].astype(F32) for s in range(CH)
+            ]
             for t in range(4 * k, min(4 * k + 4, 9)):
                 for half in range(2):
                     total = jnp.zeros((NB, LANES), F32)
@@ -562,7 +565,8 @@
             put_rows(96 * p, g1part[p] + g1swap[p])
             to_owners(4 * p, 4 * p + 4)
 
-    second_hops(hgath, hg_sems)
+    arrive(hgath, hg_sems, 2)
+    send(hgath, hg_sems, 7, 4, 5)
     turn_weights(0)
 
     def ag_copy(k, slot):
@@ -577,10 +581,7 @@
 
     @pl.when(chip < OWNERS)
     def _():
-        @pl.loop(1, PEERS)
-        def _(k):
-            rs_copy(0, lax.rem(chip + k, PEERS)).wait_recv()
-
+        all_pieces(PEERS - 1).wait_recv()
         total = rs_recv[0].astype(F32)
         for s in range(1, PEERS):
             total = total + rs_recv[s].astype(F32)
@@ -590,7 +591,7 @@
             ag_copy(k, chip).start()
         sib_copy(chip).start()
 
-    last_hops(hgath, hg_sems)
+    arrive(hgath, hg_sems, 0, 1, 3, 4, 5, 7)
     products(lhs2[0], hgath, hgath[:, ROWS], prod)
 
     @pl.loop(0, NB // group_size)
@@ -629,9 +630,8 @@
     to_left.wait_send()
     to_right.wait_send()
     w_out.wait_send()
-    g2_swap.wait_send()
     for buf, sems in ((gath.at[0], main_sems.at[0]), (gath.at[1], main_sems.at[1]), (hgath, hg_sems)):
-        for j in range(len(HOPS)):
+        for j in (0, 1, 2, 3, 4, 5, 7 if buf is hgath else 6):
             hop(buf, sems, j).wait_send()
 
     @pl.loop(1, CH)
@@ -648,10 +648,13 @@
         def _(k):
             tile_copy(k, column).wait_send()
 
-    for j in range(4):
-        @pl.when((core == 0) | (core * 4 + j != chan))
-        def _():
-            g2_sent(j).wait_send()
+    @pl.loop(1, CH)
+    def _(k):
+        g2_copy(chan_at(k), core, chan).wait_send()
+
+    @pl.when(core == 0)
+    def _():
+        g2_copy(chan, core, chan).wait_send()
 
     @pl.when(core == 1)
     def _():
@@ -664,7 +667,7 @@
 
         @pl.when(owner != chip)
         def _():
-            rs_copy(owner, chip).wait_send()
+            rs_copy(owner).wait_send()
 
     @pl.when(chip < OWNERS)
     def _():
@@ -705,10 +708,8 @@
             pltpu.VMEM((2, 3, ROWS + 2, NB, LANES), BF16),
             pltpu.VMEM((NB, LANES), F32),
             pltpu.VMEM((CH, ROWS + 1, NB, LANES), BF16),
-            pltpu.VMEM((CH, 3, NB, LANES), F32),
-            pltpu.VMEM((4, 3, NB, LANES), F32),
-            pltpu.VMEM((4, 3, NB, LANES), BF16),
             pltpu.VMEM((CH, 3, NB, LANES), BF16),
+            pltpu.VMEM((2, CH, 3, NB, LANES), BF16),
             pltpu.VMEM((3, 3 * NB, CH * NB), F32),
             pltpu.VMEM((3, 3 * NB, CH * NB), F32),
             pltpu.VMEM((2, 9 * NB, LANES), BF16),
@@ -723,10 +724,9 @@
             dma((2, 4)),
             dma((2, 1)),
             dma((2, len(HOPS))),
-            dma((2, 1)),
-            dma((2, CH)),
+            dma((2, 2, CH)),
             dma((2, 3)),
-            dma((2, PEERS)),
+            dma((2,)),
             dma((2, PEERS)),
             dma((2, OWNERS)),
         ],

time: 50.7 us -> 48.6 us (0.959)
  Pallas kernels: 48.4 us -> 46.4 us
    pallas_call x1, Pallas kernels: 48.4 us -> 46.4 us  [on_device(): pl.pallas_call(kernel, out_shape=(jax.ShapeDtypeStruct((NB, ROWS, LANES),...]
where the time goes in v5:
time: 48.6 us; the launch traced here: 48.5 us
  Pallas kernels  46.4 us (95%)
  other arithmetic  0.87 us (2%)
  between operations  0.64 us (1%)
  local copies, waits for them, and re-layouts  0.63 us (1%)
    pallas_call x1, Pallas kernels, on_device(): pl.pallas_call(kernel, out_shape=(jax.ShapeDtypeStruct((NB, ROWS, LANES),...  46.4 us

profile of v5, /device:TPU:1, one launch (start us, length us, event | category | flops | bytes accessed | tf_op | source)
XLA Modules:
  0.0 48.5 jit_solution(9021971686689030095)
XLA Ops:
  0.6 46.4 %shard_map.67 = (bf16[32,8,128]{2,1,0:T(8,128)(2,1)S(1)}, bf16[288,256]{1,0:T(8,128)(2,1)S(1)}, bf16[288,256]{1,0:T(8,128)(2,1)S(1)}) custom-call(bf16[32,8,128]{2,1,0:T(8,128)(2,1)} %field_hbm.1, bf16[9,32,256]{2,1,0:T(8,128)(2,1)} %bitcast.12, bf16[9,32,256]{2,1,0:T(8,128)(2,1)} %bitcast.13, bf16[32,8,128]{2,1,0:T(8,128)(2,1)} %cot_hbm.1), custom_call_target="tpu_custom_call" | custom-call | tf_op jit(solution)/shard_map/pallas_call | solution.py:682
  47.0 0.9 %convert_bitcast_fusion = (f32[32,9,256]{2,0,1:T(8,128)}, f32[32,9,256]{2,0,1:T(8,128)}) fusion(bf16[9,32,256]{2,1,0:T(8,128)(2,1)S(1)} %bitcast.11, bf16[9,32,256]{2,1,0:T(8,128)(2,1)S(1)} %bitcast.10), kind=kLoop, calls=%fused_computation | loop fusion | flops 147456 | bytes 884736 | tf_op jit(solution)/shard_map/transpose | solution.py:746
  47.9 0.6 %copy.8 = bf16[32,8,128]{2,1,0:T(8,128)(2,1)} copy(bf16[32,8,128]{2,1,0:T(8,128)(2,1)S(1)} %get-tuple-element.14) | data formatting | bytes 131072

commit v6 on v5

--- a/solution.py
+++ b/solution.py
@@ -36,10 +36,13 @@
     return pltpu.roll(values, amount, 1)
 
 
+def shift_main(main, ext, step):
+    wraps = lane_ids(main.shape) == (0 if step == 1 else LANES - 1)
+    return roll(jnp.where(wraps, ext, main), -step)
+
+
 def shift(main, ext, step):
-    rolled, rolled_ext = roll(main, -step), roll(ext, -step)
-    edge = lane_ids(main.shape) == (LANES - 1 if step == 1 else 0)
-    return jnp.where(edge, rolled_ext, rolled), jnp.where(edge, rolled, rolled_ext)
+    return shift_main(main, ext, step), shift_main(ext, main, step)
 
 
 def row_up(values, size):
@@ -81,20 +84,19 @@
             + jnp.where(owner == ROWS - 1, 0.0, roll(up_pack, -16))
             + jnp.where(owner == 0, 0.0, roll(down_pack, 16))
         )
+    near = (lane_ids((size, LANES)) - offset) % 16
+    from_left, from_right = roll(packs[0], 1), roll(packs[2], -1)
+    edges = jnp.where(near == 0, from_left, from_right)
+    outer = packs[1] + jnp.where(near == 0, 0.0, from_left) + jnp.where(near == 15, 0.0, from_right)
+
+    def expand(values):
+        return jnp.concatenate([roll(values, -16 * r - offset) for r in range(ROWS)], axis=0)
+
     lane = lane_ids(mains[1].shape)
-    left_edge, right_edge = lane == 0, lane == LANES - 1
-
-    def expand(values, q):
-        return jnp.concatenate([roll(values, -16 * r - q - offset) for r in range(ROWS)], axis=0)
-
-    before, before_ext = roll(mains[0], 1), expand(packs[0], -1)
-    after, after_ext = roll(mains[2], -1), expand(packs[2], 1)
-    main = mains[1] + jnp.where(left_edge, before_ext, before) + jnp.where(right_edge, after_ext, after)
-    ext = (
-        expand(packs[1], 0)
-        + jnp.where(left_edge, before, before_ext)
-        + jnp.where(right_edge, after, after_ext)
-    )
+    first, last = lane == 0, lane == LANES - 1
+    before, after, edges = roll(mains[0], 1), roll(mains[2], -1), expand(edges)
+    main = mains[1] + jnp.where(first, edges, before) + jnp.where(last, edges, after)
+    ext = expand(outer) + jnp.where(first, before, 0.0) + jnp.where(last, after, 0.0)
     return main, ext
 
 
@@ -125,15 +127,14 @@
             values.append(value)
             slopes[part, kind, :, group_rows(group, size), :] = slope.reshape(ROWS, size, LANES)
         acts.append(values)
-    left_even = shift(acts[0][1], acts[1][1], -1)
-    left_odd = shift(acts[0][3], acts[1][3], -1)
-    out = []
-    for part in range(2):
-        even = (left_even[part] + 2.0 * acts[part][0] + acts[part][1]) * 0.25
-        odd = (left_odd[part] + 2.0 * acts[part][2] + acts[part][3]) * 0.25
-        out.append(rounded((row_down(odd, size) + 2.0 * even + odd) * 0.25))
-    main, ext = out
-    store_shifted(smooth, shift(main, ext, -1)[0], main, shift(main, ext, 1)[0], group, size)
+    base, moved = [], []
+    for values in acts:
+        side = 2.0 * values[1] + values[3] + row_down(values[3], size)
+        base.append(side + 4.0 * values[0] + 2.0 * (values[2] + row_down(values[2], size)))
+        moved.append(side)
+    left, left_ext = shift(moved[0], moved[1], -1)
+    main, ext = rounded((base[0] + left) * 0.0625), rounded((base[1] + left_ext) * 0.0625)
+    store_shifted(smooth, shift_main(main, ext, -1), main, shift_main(main, ext, 1), group, size)
 
 
 def group_rows(group, size):
@@ -164,7 +165,7 @@
         moved.append(half)
     left, left_ext = shift(moved[0], moved[1], -1)
     main, ext = rounded(base[0] + left), rounded(base[1] + left_ext)
-    store_shifted(grads, shift(main, ext, 1)[0], main, shift(main, ext, -1)[0], group, size)
+    store_shifted(grads, shift_main(main, ext, 1), main, shift_main(main, ext, -1), group, size)
     packed[group_rows(group, size), :] = pack([ext[r * size : (r + 1) * size] for r in range(ROWS)])
 
 
@@ -433,6 +434,17 @@
 
     shifted[0] = shifted32[...].astype(BF16)
 
+    remote(wrecv.at[1 - core], wrecv.at[1 - core], wsib_sems, 0, space=sibling).wait_recv()
+
+    def turn_weights(which):
+        for k in range(3):
+            turned = wrecv[which, k].reshape(CH * NB, LANES).T
+            if k < 2:
+                lhs2[which, k * LANES : (k + 1) * LANES, :] = turned
+            else:
+                lhs2[which, 2 * LANES :, :] = turned[:NB]
+
+    turn_weights(1)
     last_hops(*cot_all)
     total = jnp.zeros((CH * NB, 3 * LANES), F32)
     for r in range(0, ROWS, 2):
@@ -462,17 +474,6 @@
     def _():
         g2recv[1, chan] = g2send[chan]
 
-    remote(wrecv.at[1 - core], wrecv.at[1 - core], wsib_sems, 0, space=sibling).wait_recv()
-
-    def turn_weights(which):
-        for k in range(3):
-            turned = wrecv[which, k].reshape(CH * NB, LANES).T
-            if k < 2:
-                lhs2[which, k * LANES : (k + 1) * LANES, :] = turned
-            else:
-                lhs2[which, 2 * LANES :, :] = turned[:NB]
-
-    turn_weights(1)
     products(lhs2[1], gath.at[1], halo[...], prod)
 
     @pl.loop(0, NB // group_size)

time: 48.6 us -> 48.1 us (0.990)
  Pallas kernels: 46.4 us -> 45.8 us
    pallas_call x1, Pallas kernels: 46.4 us -> 45.8 us  [on_device(): pl.pallas_call(kernel, out_shape=(jax.ShapeDtypeStruct((NB, ROWS, LANES),...]
where the time goes in v6:
time: 48.1 us; the launch traced here: 48 us
  Pallas kernels  45.8 us (95%)
  other arithmetic  0.87 us (2%)
  between operations  0.64 us (1%)
  local copies, waits for them, and re-layouts  0.63 us (1%)
    pallas_call x1, Pallas kernels, on_device(): pl.pallas_call(kernel, out_shape=(jax.ShapeDtypeStruct((NB, ROWS, LANES),...  45.8 us

profile of v6, /device:TPU:1, one launch (start us, length us, event | category | flops | bytes accessed | tf_op | source)
XLA Modules:
  0.0 48.0 jit_solution(13077097108748523979)
XLA Ops:
  0.6 45.8 %shard_map.67 = (bf16[32,8,128]{2,1,0:T(8,128)(2,1)S(1)}, bf16[288,256]{1,0:T(8,128)(2,1)S(1)}, bf16[288,256]{1,0:T(8,128)(2,1)S(1)}) custom-call(bf16[32,8,128]{2,1,0:T(8,128)(2,1)} %field_hbm.1, bf16[9,32,256]{2,1,0:T(8,128)(2,1)} %bitcast.12, bf16[9,32,256]{2,1,0:T(8,128)(2,1)} %bitcast.13, bf16[32,8,128]{2,1,0:T(8,128)(2,1)} %cot_hbm.1), custom_call_target="tpu_custom_call" | custom-call | tf_op jit(solution)/shard_map/pallas_call | solution.py:683
  46.5 0.9 %convert_bitcast_fusion = (f32[32,9,256]{2,0,1:T(8,128)}, f32[32,9,256]{2,0,1:T(8,128)}) fusion(bf16[9,32,256]{2,1,0:T(8,128)(2,1)S(1)} %bitcast.11, bf16[9,32,256]{2,1,0:T(8,128)(2,1)S(1)} %bitcast.10), kind=kLoop, calls=%fused_computation | loop fusion | flops 147456 | bytes 884736 | tf_op jit(solution)/shard_map/transpose | solution.py:747
  47.3 0.6 %copy.8 = bf16[32,8,128]{2,1,0:T(8,128)(2,1)} copy(bf16[32,8,128]{2,1,0:T(8,128)(2,1)S(1)} %get-tuple-element.14) | data formatting | bytes 131072

commit v7 on v6

--- a/solution.py
+++ b/solution.py
@@ -488,7 +488,8 @@
     def g1_copy(p):
         return remote(g1part.at[p], g1swap.at[p], g1_sems, p, space=sibling)
 
-    for p in range(3):
+    chunks = range(3)
+    for p in chunks:
         total = jnp.zeros((3 * NB, CH * NB), F32)
         for r in range(0, ROWS, 2):
             lhs = jnp.concatenate(
@@ -520,9 +521,10 @@
             device_id={"space": sibling}, device_id_type=MESH,
         )
 
-    def to_owners(low, high):
-        @pl.loop(low, high)
-        def _(owner):
+    def to_owners(p):
+        for step in range(4):
+            owner = 4 * p + lax.rem(column + (2, 1, 3, 0)[step], 4)
+
             @pl.when(owner == chip)
             def _():
                 rs_recv[PEERS - 1] = piece_of(rs_send, chip)[...]
@@ -533,7 +535,7 @@
 
     def put_rows(first, values):
         for half in range(2):
-            rs_send[half, first : first + values.shape[0]] = values[
+            rs_send[half, pl.ds(pl.multiple_of(first, 16), values.shape[0])] = values[
                 :, half * LANES : (half + 1) * LANES
             ].astype(BF16)
 
@@ -557,14 +559,15 @@
                         moved = roll(loaded[4 * half + place], (place - t % 4) * NB)
                         total = jnp.where(lane // NB == place, moved, total)
                     rs_send[half, t * NB : (t + 1) * NB] = total.astype(BF16)
-        to_owners(0, OWNERS)
+        for p in chunks:
+            to_owners(p)
 
     @pl.when(core == 0)
     def _():
-        for p in range(3):
+        for p in chunks:
             g1_copy(p).wait_recv()
             put_rows(96 * p, g1part[p] + g1swap[p])
-            to_owners(4 * p, 4 * p + 4)
+            to_owners(p)
 
     arrive(hgath, hg_sems, 2)
     send(hgath, hg_sems, 7, 4, 5)

time: 48.1 us -> 47.5 us (0.988)
  Pallas kernels: 45.8 us -> 45.2 us
    pallas_call x1, Pallas kernels: 45.8 us -> 45.2 us  [on_device(): pl.pallas_call(kernel, out_shape=(jax.ShapeDtypeStruct((NB, ROWS, LANES),...]
where the time goes in v7:
time: 47.5 us; the launch traced here: 47.4 us
  Pallas kernels  45.2 us (95%)
  other arithmetic  0.87 us (2%)
  between operations  0.64 us (1%)
  local copies, waits for them, and re-layouts  0.63 us (1%)
    pallas_call x1, Pallas kernels, on_device(): pl.pallas_call(kernel, out_shape=(jax.ShapeDtypeStruct((NB, ROWS, LANES),...  45.2 us

profile of v7, /device:TPU:1, one launch (start us, length us, event | category | flops | bytes accessed | tf_op | source)
XLA Modules:
  0.0 47.4 jit_solution(9880707835021428256)
XLA Ops:
  0.6 45.2 %shard_map.67 = (bf16[32,8,128]{2,1,0:T(8,128)(2,1)S(1)}, bf16[288,256]{1,0:T(8,128)(2,1)S(1)}, bf16[288,256]{1,0:T(8,128)(2,1)S(1)}) custom-call(bf16[32,8,128]{2,1,0:T(8,128)(2,1)} %field_hbm.1, bf16[9,32,256]{2,1,0:T(8,128)(2,1)} %bitcast.12, bf16[9,32,256]{2,1,0:T(8,128)(2,1)} %bitcast.13, bf16[32,8,128]{2,1,0:T(8,128)(2,1)} %cot_hbm.1), custom_call_target="tpu_custom_call" | custom-call | tf_op jit(solution)/shard_map/pallas_call | solution.py:686
  45.9 0.9 %convert_bitcast_fusion = (f32[32,9,256]{2,0,1:T(8,128)}, f32[32,9,256]{2,0,1:T(8,128)}) fusion(bf16[9,32,256]{2,1,0:T(8,128)(2,1)S(1)} %bitcast.11, bf16[9,32,256]{2,1,0:T(8,128)(2,1)S(1)} %bitcast.10), kind=kLoop, calls=%fused_computation | loop fusion | flops 147456 | bytes 884736 | tf_op jit(solution)/shard_map/transpose | solution.py:750
  46.7 0.6 %copy.8 = bf16[32,8,128]{2,1,0:T(8,128)(2,1)} copy(bf16[32,8,128]{2,1,0:T(8,128)(2,1)S(1)} %get-tuple-element.14) | data formatting | bytes 131072

commit v8 on v7

--- a/solution.py
+++ b/solution.py
@@ -205,6 +205,8 @@
     key=lambda d: (2 * min(d[0], 4 - d[0]) + min(d[1], 4 - d[1]), d),
 )
 
+FARTHEST = (4, 3, 5, 2, 6, 1, 7)
+
 HOPS = (
     ((0, 0), (1, 0), (-1, 0)),
     ((0, 0), (-1, 0), (1, 0)),
@@ -364,8 +366,7 @@
 
     @pl.when(column < 3)
     def _():
-        @pl.loop(1, CH)
-        def _(k):
+        for k in FARTHEST:
             w_copy(k, chan_at(k), chan).start()
 
     field_all, cot_all = (gath.at[0], main_sems.at[0]), (gath.at[1], main_sems.at[1])
@@ -382,8 +383,7 @@
     def halo_copy(k, slot):
         return remote(halo.at[slot], halo.at[slot], halo_sems, k, chan=chan_at(k))
 
-    @pl.loop(1, CH)
-    def _(k):
+    for k in FARTHEST:
         halo_copy(k, chan).start()
 
     def tile_copy(k, tile):
@@ -402,8 +402,7 @@
         def _(k):
             w_copy(k, chan_at(k), chan_at(CH - k)).wait_recv()
 
-        @pl.loop(1, 4)
-        def _(k):
+        for k in (2, 1, 3):
             tile_copy(k, column).start()
 
     second_hops(*cot_all)
@@ -462,8 +461,7 @@
             device_id={"chan": dest, "space": 2 * chip + 1}, device_id_type=MESH,
         )
 
-    @pl.loop(1, CH)
-    def _(k):
+    for k in FARTHEST:
         g2_copy(chan_at(k), core, chan).start()
 
     @pl.when(core == 0)

time: 47.5 us -> 48.1 us (1.013)
  Pallas kernels: 45.2 us -> 45.8 us
    pallas_call x1, Pallas kernels: 45.2 us -> 45.8 us  [on_device(): pl.pallas_call(kernel, out_shape=(jax.ShapeDtypeStruct((NB, ROWS, LANES),...]
where the time goes in v8:
time: 48.1 us; the launch traced here: 48 us
  Pallas kernels  45.8 us (95%)
  other arithmetic  0.87 us (2%)
  between operations  0.64 us (1%)
  local copies, waits for them, and re-layouts  0.63 us (1%)
    pallas_call x1, Pallas kernels, on_device(): pl.pallas_call(kernel, out_shape=(jax.ShapeDtypeStruct((NB, ROWS, LANES),...  45.8 us

profile of v8, /device:TPU:1, one launch (start us, length us, event | category | flops | bytes accessed | tf_op | source)
XLA Modules:
  0.0 48.0 jit_solution(6880361924556919694)
XLA Ops:
  0.6 45.8 %shard_map.67 = (bf16[32,8,128]{2,1,0:T(8,128)(2,1)S(1)}, bf16[288,256]{1,0:T(8,128)(2,1)S(1)}, bf16[288,256]{1,0:T(8,128)(2,1)S(1)}) custom-call(bf16[32,8,128]{2,1,0:T(8,128)(2,1)} %field_hbm.1, bf16[9,32,256]{2,1,0:T(8,128)(2,1)} %bitcast.12, bf16[9,32,256]{2,1,0:T(8,128)(2,1)} %bitcast.13, bf16[32,8,128]{2,1,0:T(8,128)(2,1)} %cot_hbm.1), custom_call_target="tpu_custom_call" | custom-call | tf_op jit(solution)/shard_map/pallas_call | solution.py:684
  46.5 0.9 %convert_bitcast_fusion = (f32[32,9,256]{2,0,1:T(8,128)}, f32[32,9,256]{2,0,1:T(8,128)}) fusion(bf16[9,32,256]{2,1,0:T(8,128)(2,1)S(1)} %bitcast.11, bf16[9,32,256]{2,1,0:T(8,128)(2,1)S(1)} %bitcast.10), kind=kLoop, calls=%fused_computation | loop fusion | flops 147456 | bytes 884736 | tf_op jit(solution)/shard_map/transpose | solution.py:748
  47.3 0.6 %copy.8 = bf16[32,8,128]{2,1,0:T(8,128)(2,1)} copy(bf16[32,8,128]{2,1,0:T(8,128)(2,1)S(1)} %get-tuple-element.14) | data formatting | bytes 131072

commit v9 on v7

--- a/solution.py
+++ b/solution.py
@@ -382,8 +382,7 @@
     def halo_copy(k, slot):
         return remote(halo.at[slot], halo.at[slot], halo_sems, k, chan=chan_at(k))
 
-    @pl.loop(1, CH)
-    def _(k):
+    for k in (4, 3, 5, 2, 6, 1, 7):
         halo_copy(k, chan).start()
 
     def tile_copy(k, tile):

time: 47.5 us -> 47.5 us (level)
  no operation moved by 1% of the time
where the time goes in v9:
time: 47.5 us; the launch traced here: 47.4 us
  Pallas kernels  45.2 us (95%)
  other arithmetic  0.87 us (2%)
  between operations  0.64 us (1%)
  local copies, waits for them, and re-layouts  0.63 us (1%)
    pallas_call x1, Pallas kernels, on_device(): pl.pallas_call(kernel, out_shape=(jax.ShapeDtypeStruct((NB, ROWS, LANES),...  45.2 us

profile of v9, /device:TPU:1, one launch (start us, length us, event | category | flops | bytes accessed | tf_op | source)
XLA Modules:
  0.0 47.4 jit_solution(14561813349193829707)
XLA Ops:
  0.6 45.2 %shard_map.67 = (bf16[32,8,128]{2,1,0:T(8,128)(2,1)S(1)}, bf16[288,256]{1,0:T(8,128)(2,1)S(1)}, bf16[288,256]{1,0:T(8,128)(2,1)S(1)}) custom-call(bf16[32,8,128]{2,1,0:T(8,128)(2,1)} %field_hbm.1, bf16[9,32,256]{2,1,0:T(8,128)(2,1)} %bitcast.12, bf16[9,32,256]{2,1,0:T(8,128)(2,1)} %bitcast.13, bf16[32,8,128]{2,1,0:T(8,128)(2,1)} %cot_hbm.1), custom_call_target="tpu_custom_call" | custom-call | tf_op jit(solution)/shard_map/pallas_call | solution.py:685
  45.9 0.9 %convert_bitcast_fusion = (f32[32,9,256]{2,0,1:T(8,128)}, f32[32,9,256]{2,0,1:T(8,128)}) fusion(bf16[9,32,256]{2,1,0:T(8,128)(2,1)S(1)} %bitcast.11, bf16[9,32,256]{2,1,0:T(8,128)(2,1)S(1)} %bitcast.10), kind=kLoop, calls=%fused_computation | loop fusion | flops 147456 | bytes 884736 | tf_op jit(solution)/shard_map/transpose | solution.py:749
  46.7 0.6 %copy.8 = bf16[32,8,128]{2,1,0:T(8,128)(2,1)} copy(bf16[32,8,128]{2,1,0:T(8,128)(2,1)S(1)} %get-tuple-element.14) | data formatting | bytes 131072
